TPU v7x, 128 devices: a whole 4x4x4 slice. The times are simulated.
128 devices in a mesh: replica: 8 (over y, core), group: 16 (over x, z).
Axes of the slice: x: 4, y: 4, z: 4, core: 2. Of those that a mesh axis runs over, the one named last changes fastest.
Arguments:
- layer_input: bfloat16 [98304, 4096], P(('replica', 'group')), may hold values from -50 to 50
- up_cotangent: bfloat16 [98304, 1792], P(('replica', 'group')), may hold values from -1.5 to 1.5
- attn_values: bfloat16 [98304, 512], P(('replica', 'group')), may hold values from -6 to 6
- resid_cotangent: bfloat16 [98304, 4096], P(('replica', 'group')), may hold values from -12.5 to 12.5
- feedback: float32 [8, 4096, 2304], P('replica', 'group'), may hold values from -6 to 6
- start_seed: int32 [1], replicated, may hold values from 0 to 999999
Outputs:
- update: bfloat16 [4096, 2304], P(None, 'replica')
- new_feedback: float32 [8, 4096, 2304], P('replica', 'group')
All inputs are finite; a program needn't handle non-finite values.
Results may differ from a plain program's by a relative error of at most 0.001.
Values may be sent and summed in bfloat16 or wider, within the bound.
A program may use at most 256 MiB of HBM per device.

v0:
```python
import jax
import jax.numpy as jnp
from jax import lax
from jax.sharding import PartitionSpec as P

RANK = 32


def make_factor(start_seed, count, layer):
    positions = jnp.arange(count, dtype=jnp.int32)[:, None]
    columns = jnp.arange(RANK, dtype=jnp.int32)[None, :]
    base = start_seed[0] % 65521
    mixed = (base * 31 + positions * 977 + columns * 7919 + layer * 4099 + 12345) % 65521
    folded = mixed % 256 * (mixed // 256) % 65521
    final = (folded * 181 + mixed) % 65521
    return (final.astype(jnp.float32) / 65521.0 - 0.5) * 3.4


def highest(left, right):
    return jnp.dot(left, right, precision=lax.Precision.HIGHEST)


def solve_lower(lower, target):
    return jax.scipy.linalg.solve_triangular(lower, target.T, lower=True).T


def on_device(layer_input, up_cotangent, attn_values, resid_cotangent, feedback, start_seed):
    groups = lax.axis_size("group")
    replicas = lax.axis_size("replica")
    width_up = up_cotangent.shape[1]
    width_attn = attn_values.shape[1]
    first = jnp.einsum("td,tf->df", layer_input, up_cotangent, preferred_element_type=jnp.float32)
    second = jnp.einsum(
        "td,th->dh", resid_cotangent, attn_values, preferred_element_type=jnp.float32
    )
    summed = lax.psum_scatter(
        jnp.concatenate([first, second], axis=1), "group", scatter_dimension=0, tiled=True
    )
    matrix = summed / groups + feedback[0]
    left_block = matrix[:, :width_up]
    right_block = matrix[:, width_up:]
    factor_left = make_factor(start_seed, width_up, 0)
    factor_right = make_factor(start_seed, width_attn, 1)
    mean_left, mean_right = lax.psum(
        (highest(left_block, factor_left), highest(right_block, factor_right)), "replica"
    )
    mean_left = mean_left / replicas
    mean_right = mean_right / replicas
    gram_left, gram_right = lax.psum(
        (highest(mean_left.T, mean_left), highest(mean_right.T, mean_right)), "group"
    )
    basis_left = solve_lower(jnp.linalg.cholesky(gram_left), mean_left)
    basis_right = solve_lower(jnp.linalg.cholesky(gram_right), mean_right)
    back_left, back_right = lax.psum(
        (highest(left_block.T, basis_left), highest(right_block.T, basis_right)), "group"
    )
    back_left, back_right = lax.psum((back_left, back_right), "replica")
    back_left = back_left / replicas
    back_right = back_right / replicas
    approx = jnp.concatenate(
        [highest(basis_left, back_left.T), highest(basis_right, back_right.T)], axis=1
    )
    new_feedback = (matrix - approx)[None]
    width_out = approx.shape[1] // replicas
    piece = lax.dynamic_slice_in_dim(
        approx, lax.axis_index("replica") * width_out, width_out, 1
    ).astype(jnp.bfloat16)
    update = lax.all_gather(piece, "group", axis=0, tiled=True)
    return (update, new_feedback)


def solution(mesh):
    in_specs = (
        P(("replica", "group"), None),
        P(("replica", "group"), None),
        P(("replica", "group"), None),
        P(("replica", "group"), None),
        P("replica", "group", None),
        P(),
    )
    out_specs = (P(None, "replica"), P("replica", "group", None))
    return jax.shard_map(
        on_device, mesh=mesh, in_specs=in_specs, out_specs=out_specs, check_vma=False
    )
```

profile of v0, /device:TPU:0, one launch (start us, length us, event | category | flops | bytes accessed | tf_op | source)
XLA Modules:
  0.0 653.8 jit_solution(12035614939376880696)
XLA Ops:
  7.2 0.0 copy-start
  7.2 0.0 copy-start.5
  7.2 0.0 reduce-scatter.2.cloned.1.call-start
  7.2 1.7 copy-done
  8.9 0.0 copy-start.4
  9.0 19.9 %fusion.150 = f32[4096,1792]{0,1:T(8,128)} fusion(bf16[768,4096]{1,0:T(8,128)(2,1)} %param.9, bf16[768,1792]{1,0:T(8,128)(2,1)S(1)} %copy-done), kind=kOutput, calls=%fused_computation.180 | convolution fusion | flops 11274289152 | bytes 38404096 | tf_op jit(solution)/shard_map/td,tf->df/dot_general | solution.py:32
  28.8 0.0 copy-done.5
  28.8 0.0 copy-done.4
  28.8 6.0 fusion.151
  34.8 26.1 %pad_maximum_fusion = f32[4096,2304]{0,1:T(8,128)} fusion(f32[4096,512]{0,1:T(8,128)} %fusion.151, f32[4096,1792]{0,1:T(8,128)} %fusion.150), kind=kLoop, calls=%fused_computation | loop fusion | flops 9437184 | bytes 75497472 | tf_op jit(solution)/shard_map/concatenate | solution.py:37
  61.0 0.0 copy-start.3
  61.0 0.0 reduce-scatter.2.cloned.1.call-update
  61.0 0.2 all-reduce.10.cloned.1.call-start
  62.0 0.6 copy-done.3
  62.6 1.9 copy.8
  64.6 215.0 %reduce-scatter.2.cloned.1.call-done = f32[256,2304]{0,1:T(8,128)} async-done(((f32[4096,2304]{0,1:T(8,128)}), f32[256,2304]{0,1:T(8,128)}) %reduce-scatter.2.cloned.1.call-update) | async-done | bytes 2359312 | tf_op jit(solution)/shard_map/reduce_scatter | solution.py:36
  279.6 2.7 bitcast_add_fusion
  282.3 4.7 fusion.4
  287.0 1.9 fusion.37
  288.9 0.0 all-reduce.10.cloned.1.call-update
  288.9 0.0 all-reduce.8.cloned.1.call-start
  288.9 58.6 %all-reduce.10.cloned.1.call-done = (f32[256,32]{0,1:T(8,128)}, f32[256,32]{0,1:T(8,128)}) async-done(((f32[256,32]{0,1:T(8,128)}, f32[256,32]{0,1:T(8,128)}), (f32[256,32]{0,1:T(8,128)}, f32[256,32]{0,1:T(8,128)})) %all-reduce.10.cloned.1.call-update) | async-done | bytes 65552 | tf_op jit(solution)/shard_map/psum | solution.py:44
  347.5 1.0 fusion.105
  348.5 1.0 fusion.108
  349.5 74.5 %all-reduce = (f32[32,32]{0,1:T(8,128)S(1)}, f32[32,32]{0,1:T(8,128)S(1)}) all-reduce(f32[32,32]{0,1:T(8,128)S(1)} %fusion.108, f32[32,32]{0,1:T(8,128)S(1)} %fusion.105), channel_id=1, replica_groups=mesh['replica'=8,'group'=16] {'group'}, use_global_device_ids=true, to_apply=%region_2.3 | all-reduce | flops 2048 | bytes 16384 | tf_op jit(solution)/shard_map/psum | solution.py:49
  424.0 0.1 copy.10
  424.1 0.1 copy.12
  424.1 2.9 cholesky.55
  427.1 0.6 compare_reduce_fusion
  427.7 0.7 fusion.111
  428.4 2.5 custom-call.7
  430.9 1.0 fusion.100
  431.8 1.3 fusion.35
  433.1 2.9 cholesky.44
  436.0 0.6 compare_reduce_fusion.1
  436.7 0.7 fusion.110
  437.3 2.5 custom-call.6
  439.8 1.0 fusion.102
  440.8 2.5 fusion.2
  443.3 0.0 all-reduce.8.cloned.1.call-update
  443.3 0.0 all-reduce.12.cloned.1.call-start
  443.4 81.0 %all-reduce.8.cloned.1.call-done = (f32[1792,32]{1,0:T(8,128)}, f32[512,32]{1,0:T(8,128)}) async-done(((f32[1792,32]{1,0:T(8,128)}, f32[512,32]{1,0:T(8,128)}), (f32[1792,32]{1,0:T(8,128)}, f32[512,32]{1,0:T(8,128)})) %all-reduce.8.cloned.1.call-update) | async-done | bytes 294928 | tf_op jit(solution)/shard_map/psum | solution.py:54
  524.4 0.0 all-reduce.12.cloned.1.call-update
  524.4 0.3 all-gather.2.cloned.1.call-start
  524.7 64.4 %all-reduce.12.cloned.1.call-done = (f32[1792,32]{1,0:T(8,128)}, f32[512,32]{1,0:T(8,128)}) async-done(((f32[1792,32]{1,0:T(8,128)}, f32[512,32]{1,0:T(8,128)}), (f32[1792,32]{1,0:T(8,128)}, f32[512,32]{1,0:T(8,128)})) %all-reduce.12.cloned.1.call-update) | async-done | bytes 294928 | tf_op jit(solution)/shard_map/psum | solution.py:57
  589.1 1.5 fusion.66
  590.6 2.7 fusion.16
  593.4 0.0 copy-start.2
  593.4 1.2 copy-done.2
  594.6 0.7 fusion.55
  595.4 0.0 all-gather.2.cloned.1.call-update
  595.4 3.2 fusion.1
  598.6 0.0 copy-start.1
  598.6 3.2 copy.15
  601.8 42.1 %all-gather.2.cloned.1.call-done = bf16[4096,288]{0,1:T(8,128)(2,1)} async-done(((bf16[256,288]{0,1:T(8,128)(2,1)}), bf16[4096,288]{0,1:T(8,128)(2,1)}) %all-gather.2.cloned.1.call-update) | async-done | bytes 2359312 | tf_op jit(solution)/shard_map/all_gather | solution.py:68
  643.9 3.3 copy.28
  647.2 0.0 copy-done.1
  (6 shorter events, 0.1 us)
Async XLA Ops:
  7.2 1.8 copy-start
  7.2 21.6 %copy-start.5 = (bf16[768,512]{1,0:T(8,128)(2,1)S(1)}, bf16[768,512]{1,0:T(8,128)(2,1)}, u32[]{:S(2)}) copy-start(bf16[768,512]{1,0:T(8,128)(2,1)} %param.11) | copy-start | bytes 2359300
  7.2 272.4 %reduce-scatter.2.cloned.1.call-start = ((), (), s32[]{:S(2)}) async-start(), calls=%async_computation.1 | async-start | bytes 40108032 | tf_op jit(solution)/shard_map/reduce_scatter | solution.py:36
  8.9 19.9 %copy-start.4 = (bf16[768,4096]{1,0:T(8,128)(2,1)S(1)}, bf16[768,4096]{1,0:T(8,128)(2,1)}, u32[]{:S(2)}) copy-start(bf16[768,4096]{1,0:T(8,128)(2,1)} %param.12) | copy-start | bytes 18874372
  61.0 1.7 copy-start.3
  61.0 286.5 %all-reduce.10.cloned.1.call-start = ((), (), s32[]{:S(2)}) async-start(), calls=%async_computation.4 | async-start | bytes 131072 | tf_op jit(solution)/shard_map/psum | solution.py:44
  288.9 235.5 %all-reduce.8.cloned.1.call-start = ((), (), s32[]{:S(2)}) async-start(), calls=%async_computation.3 | async-start | bytes 2359296 | tf_op jit(solution)/shard_map/psum | solution.py:54
  443.3 145.8 %all-reduce.12.cloned.1.call-start = ((), (), s32[]{:S(2)}) async-start(), calls=%async_computation.5 | async-start | bytes 2359296 | tf_op jit(solution)/shard_map/psum | solution.py:57
  524.4 119.5 %all-gather.2.cloned.1.call-start = ((), (), s32[]{:S(2)}) async-start(), calls=%async_computation.2 | async-start | bytes 2506752 | tf_op jit(solution)/shard_map/all_gather | solution.py:68
  593.4 1.2 copy-start.2
  598.6 48.6 %copy-start.1 = (bf16[768,1792]{1,0:T(8,128)(2,1)S(1)}, bf16[768,1792]{1,0:T(8,128)(2,1)}, u32[]{:S(2)}) copy-start(bf16[768,1792]{1,0:T(8,128)(2,1)} %param.10) | copy-start | bytes 8257540
Sparse Core Ops, SparseCore 0:
  61.1 218.4 reduce-scatter.1
  289.0 58.4 all-reduce.9
  443.4 80.9 all-reduce.7
  526.9 62.1 all-reduce.11
  595.5 48.3 all-gather.1
where the time goes:
time: 654 us
  waiting for transfers between devices  461 us (70%)
  blocking collectives  74.5 us (11%)
  other arithmetic  46.2 us (7%)
  matrix products  44.4 us (7%)
  between operations  14.7 us (2%)
  local copies, waits for them, and re-layouts  12.2 us (2%)
    reduce_scatter x1, waiting for transfers between devices, on_device(): lax.psum_scatter(jnp.concatenate([first, second], axis=1), 'group', scatt...  215 us
    psum x1, waiting for transfers between devices, on_device(): lax.psum((highest(left_block.T, basis_left), highest(right_block.T, basis...  81 us
    psum x1, blocking collectives, on_device(): lax.psum((highest(mean_left.T, mean_left), highest(mean_right.T, mean_rig...  74.5 us
    psum x1, waiting for transfers between devices, on_device(): back_left, back_right = lax.psum((back_left, back_right), 'replica')  64.4 us
    psum x1, waiting for transfers between devices, on_device(): lax.psum((highest(left_block, factor_left), highest(right_block, factor_r...  58.6 us
    all_gather x1, waiting for transfers between devices, on_device(): update = lax.all_gather(piece, 'group', axis=0, tiled=True)  42.1 us
    concatenate x1, other arithmetic, on_device(): jnp.concatenate([first, second], axis=1)  26.1 us
    dot_general x1, matrix products, on_device(): jnp.einsum('td,tf->df', layer_input, up_cotangent, preferred_element_type...  19.9 us
  transfers between devices with their start and end apart: 5, of which 5 were waited for; matrix products, arithmetic and copies ran while one was open for 1% of the time, Pallas kernels for 0%

commit v1 on v0

v1 whole, which is shorter than its diff:
```python
import jax
import jax.numpy as jnp
from jax import lax
from jax.experimental import pallas as pl
from jax.experimental.pallas import tpu as pltpu
from jax.sharding import PartitionSpec as P

RANK = 32
TOK = 768
D = 4096
FF = 1792
HD = 512
W = FF + HD
HALF = W // 2
ROWS = 256
SIDE = 4
GROUP = 16
REP = 8
BLEN = 2048
LEVELS = 32700.0
ORDER = (2, 1, 3, 0)
MESH = pl.DeviceIdType.MESH
F32 = jnp.float32
BF16 = jnp.bfloat16
OPP_A, OPP_B, PURE_B, PURE_A, DEP_A, DEP_B = range(6)
RIGHTWARD = (True, False, True, False, True, False)


def make_factor_t(start_seed, count, layer):
    positions = jnp.arange(count, dtype=jnp.int32)[None, :]
    columns = jnp.arange(RANK, dtype=jnp.int32)[:, None]
    base = start_seed[0] % 65521
    mixed = (base * 31 + positions * 977 + columns * 7919 + layer * 4099 + 12345) % 65521
    folded = mixed % 256 * (mixed // 256) % 65521
    final = (folded * 181 + mixed) % 65521
    return (final.astype(F32) / 65521.0 - 0.5) * 3.4


def split3(v):
    hi = v.astype(BF16)
    rest = v - hi.astype(F32)
    mid = rest.astype(BF16)
    low = (rest - mid.astype(F32)).astype(BF16)
    return jnp.concatenate([hi, mid, low], axis=0)


def split2(v):
    hi = v.astype(BF16)
    return hi, (v - hi.astype(F32)).astype(BF16)


def fold3(v):
    return (v[64:96] + v[32:64]) + v[0:32]


def dot_nn(a, b):
    return lax.dot_general(a, b, (((1,), (0,)), ((), ())), preferred_element_type=F32)


def dot_nt(a, b):
    return lax.dot_general(a, b, (((1,), (1,)), ((), ())), preferred_element_type=F32)


def dot_nn_full(a, b):
    return lax.dot_general(
        a, b, (((1,), (0,)), ((), ())), precision=lax.Precision.HIGHEST, preferred_element_type=F32
    )


def dot_nt_full(a, b):
    return lax.dot_general(
        a, b, (((1,), (1,)), ((), ())), precision=lax.Precision.HIGHEST, preferred_element_type=F32
    )


def peak8(v):
    return jnp.max(jnp.abs(v).reshape(v.shape[0] // 8, 8, v.shape[1]), axis=0)


def at(start, size, step):
    return pl.ds(pl.multiple_of(start, step), size)


def inverse_factor(gram):
    row = lax.broadcasted_iota(jnp.int32, (RANK, RANK), 0)
    lane = lax.broadcasted_iota(jnp.int32, (RANK, RANK), 1)
    eye = jnp.where(row == lane, 1.0, 0.0).astype(F32)

    def step(j, state):
        out = []
        for a, b in state:
            col = jnp.sum(jnp.where(lane == j, a, 0.0), axis=1, keepdims=True)
            a_row = jnp.sum(jnp.where(row == j, a, 0.0), axis=0, keepdims=True)
            b_row = jnp.sum(jnp.where(row == j, b, 0.0), axis=0, keepdims=True)
            pivot = jnp.sum(jnp.where((row == j) & (lane == j), a, 0.0), axis=(0, 1), keepdims=True)
            factor = jnp.where(row[:, :1] > j, col / pivot, 0.0)
            out.append((a - factor * a_row, b - factor * b_row))
        return tuple(out)

    state = lax.fori_loop(0, RANK, step, tuple((g, eye) for g in gram))
    result = []
    for a, b in state:
        diag = jnp.sum(jnp.where(row == lane, a, 0.0), axis=1, keepdims=True)
        result.append(b * (1.0 / jnp.sqrt(diag)))
    return result


def kernel(
    x_hbm, u_hbm, a_hbm, g_hbm, fb_hbm, qt_ref,
    new_hbm, upd_hbm,
    xs, gs, ut, ustg, tmp, pdep, pown, tx, rx, fb,
    pt, prx, psum, prx2, psl, pg, pall,
    bt, brx, bsum, brx2, bsl, bg, ball, bk4, uout,
    load_x, load_g, load_u, load_fb, out_sem,
    tx_sem, rx_sem, small_tx, small_rx,
):
    group = lax.axis_index("group")
    rep = lax.axis_index("replica")
    gx = group // SIDE
    gz = group % SIDE

    def member(dx, dz):
        return (gx + dx) % SIDE * SIDE + (gz + dz) % SIDE

    ucopies = []
    for t in range(9):
        src = u_hbm.at[:, pl.ds(256 * t, 256)] if t < 7 else a_hbm.at[:, pl.ds(256 * (t - 7), 256)]
        ucopies.append(pltpu.make_async_copy(src, ustg.at[t % 2], load_u.at[t % 2]))
    ucopies[0].start()
    ucopies[1].start()
    steps = [(df, ds) for ds in ORDER for df in ORDER]
    for i, (df, ds) in enumerate(steps):
        low = at(ROWS * member(df, ds), 128, 128)
        high = at(ROWS * member(ds, df) + 128, 128, 128)
        pltpu.make_async_copy(x_hbm.at[:, low], xs.at[i, :, pl.ds(0, 128)], load_x.at[i]).start()
        pltpu.make_async_copy(x_hbm.at[:, high], xs.at[i, :, pl.ds(128, 128)], load_x.at[i]).start()
        pltpu.make_async_copy(g_hbm.at[:, low], gs.at[i, :, pl.ds(0, 128)], load_g.at[i]).start()
        pltpu.make_async_copy(g_hbm.at[:, high], gs.at[i, :, pl.ds(128, 128)], load_g.at[i]).start()
    pltpu.make_async_copy(fb_hbm, fb, load_fb).start()

    loaded = set()

    def wait_step(i):
        if i in loaded:
            return
        loaded.add(i)
        pltpu.make_async_copy(xs.at[i], xs.at[i], load_x.at[i]).wait()
        pltpu.make_async_copy(gs.at[i], gs.at[i], load_g.at[i]).wait()

    barrier = pltpu.get_barrier_semaphore()

    @pl.loop(1, GROUP)
    def _(d):
        pl.semaphore_signal(barrier, inc=1, device_id={"group": (group + d) % GROUP}, device_id_type=MESH)

    @pl.loop(1, REP)
    def _(d):
        pl.semaphore_signal(barrier, inc=1, device_id={"replica": (rep + d) % REP}, device_id_type=MESH)

    for t in range(9):
        ucopies[t].wait()
        ut[256 * t : 256 * t + 256, :] = ustg[t % 2].T
        if t + 2 < 9:
            ucopies[t + 2].start()

    def matmul(i, first, dst, base):
        def tile(source, size, start, to):
            r = dot_nn(ut[at(start, size, 64), :], source[i])
            dst[at(to, size, 64), :] = r
            return peak8(r)

        zero = jnp.zeros((8, ROWS), F32)
        if first:
            return lax.fori_loop(
                0, 3, lambda t, m: jnp.maximum(m, tile(xs, 384, t * 384, base + t * 384)), zero
            )
        m = lax.fori_loop(
            0, 2, lambda t, m: jnp.maximum(m, tile(xs, 320, HALF + t * 320, base + t * 320)), zero
        )
        return lax.fori_loop(
            0, 2, lambda t, m: jnp.maximum(m, tile(gs, 256, FF + t * 256, base + 640 + t * 256)), m
        )

    def quantise(src, base, m, slot):
        peak = jnp.maximum(jnp.max(m, axis=0, keepdims=True), 1e-30)
        power = jnp.ceil(jnp.log2(peak))
        scale = jnp.exp2(-power) * LEVELS

        @pl.loop(0, HALF // 64)
        def _(t):
            v = src[at(base + t * 64, 64, 64), :] * scale
            tx[slot, at(t * 64, 64, 64), :] = jnp.round(v).astype(jnp.int32).astype(jnp.int16)

        tx[slot, HALF : HALF + 16, :] = jnp.broadcast_to(power, (16, ROWS)).astype(jnp.int32).astype(jnp.int16)

    def copy_of(slot, mid, kind, stage, h):
        lanes = pl.ds(128 * h, 128)
        along_x = (h == 0) == (stage == 0)
        step = 1 if RIGHTWARD[kind] else SIDE - 1
        peer = member(step, 0) if along_x else member(0, step)
        return pltpu.make_async_remote_copy(
            src_ref=tx.at[slot, :, lanes],
            dst_ref=rx.at[mid, :, lanes],
            send_sem=tx_sem.at[mid, h],
            recv_sem=rx_sem.at[mid, h],
            device_id={"group": peer},
            device_id_type=MESH,
        )

    def slot_of(mid):
        chunk, kind = divmod(mid, 6)
        if chunk == 4:
            return 8 + kind
        return kind + (6 if chunk % 2 and kind < 2 else 0)

    def copies(mid):
        chunk, kind = divmod(mid, 6)
        return [copy_of(slot_of(mid), mid, kind, chunk // 4, h) for h in range(2)]

    pending = {}

    def send(mid, src, base, m):
        slot = slot_of(mid)
        if slot in pending:
            for c in copies(pending[slot]):
                c.wait_send()
        quantise(src, base, m, slot)
        for c in copies(mid):
            c.start()
        pending[slot] = mid

    def combine(acc, base, mids):
        for mid in mids:
            for c in copies(mid):
                c.wait_recv()
        scales = [
            jnp.exp2(rx[mid, HALF : HALF + 16, :].astype(jnp.int32).astype(F32)[:8]) * (1.0 / LEVELS)
            for mid in mids
        ]

        def tile(t, m):
            v = acc[at(base + t * 64, 64, 64), :].reshape(8, 8, ROWS)
            for mid, scale in zip(mids, scales):
                got = rx[mid, at(t * 64, 64, 64), :].astype(jnp.int32).astype(F32).reshape(8, 8, ROWS)
                v = v + got * scale[None]
            acc[at(base + t * 64, 64, 64), :] = v.reshape(64, ROWS)
            return jnp.maximum(m, jnp.max(jnp.abs(v), axis=0))

        return lax.fori_loop(0, HALF // 64, tile, jnp.zeros((8, ROWS), F32))

    def opposite(k):
        wait_step(4 * k)
        m = matmul(4 * k, True, tmp, 0)
        send(6 * k + OPP_A, tmp, 0, m)
        m = matmul(4 * k, False, tmp, 0)
        send(6 * k + OPP_B, tmp, 0, m)

    def pure(k):
        wait_step(4 * k + 1)
        m = matmul(4 * k + 1, False, tmp, 0)
        send(6 * k + PURE_B, tmp, 0, m)
        wait_step(4 * k + 2)
        m = matmul(4 * k + 2, True, tmp, 0)
        send(6 * k + PURE_A, tmp, 0, m)
        matmul(4 * k + 1, True, pdep, 0)
        matmul(4 * k + 2, False, pdep, HALF)

    def own(k):
        wait_step(4 * k + 3)
        matmul(4 * k + 3, True, pown, 0)
        matmul(4 * k + 3, False, pown, HALF)

    def dependent(k):
        m = combine(pdep, 0, [6 * k + OPP_A])
        send(6 * k + DEP_A, pdep, 0, m)
        m = combine(pdep, HALF, [6 * k + OPP_B])
        send(6 * k + DEP_B, pdep, HALF, m)

    def complete(k):
        more_a = {0: [], 1: [24 + OPP_A], 2: [], 3: [24 + DEP_A, 24 + PURE_A]}[k]
        more_b = {0: [], 1: [], 2: [24 + OPP_B], 3: [24 + PURE_B, 24 + DEP_B]}[k]
        kind_a = {0: OPP_A, 1: DEP_A, 2: PURE_A}.get(k)
        kind_b = {0: OPP_B, 1: PURE_B, 2: DEP_B}.get(k)
        m = combine(pown, 0, [6 * k + DEP_A, 6 * k + PURE_A] + more_a)
        if k < 3:
            send(24 + kind_a, pown, 0, m)
        m = combine(pown, HALF, [6 * k + PURE_B, 6 * k + DEP_B] + more_b)
        if k < 3:
            send(24 + kind_b, pown, HALF, m)

    def rep_scatter_copy(src, dst, d, which):
        peer = (rep + d) % REP
        return pltpu.make_async_remote_copy(
            src_ref=src.at[at(peer * 8, 8, 8), :],
            dst_ref=dst.at[d - 1],
            send_sem=small_tx.at[which],
            recv_sem=small_rx.at[which],
            device_id={"replica": peer},
            device_id_type=MESH,
        )

    def rep_scatter(src, dst, which):
        @pl.loop(1, REP)
        def _(d):
            rep_scatter_copy(src, dst, d, which).start()

    def group_scatter(src, dst, which):
        width = src.shape[1] // GROUP

        @pl.loop(1, GROUP)
        def _(d):
            peer = (group + d) % GROUP
            pltpu.make_async_remote_copy(
                src_ref=src.at[:, at(peer * width, width, 128)],
                dst_ref=dst.at[d - 1],
                send_sem=small_tx.at[which],
                recv_sem=small_rx.at[which],
                device_id={"group": peer},
                device_id_type=MESH,
            ).start()

    def group_gather(src, dst, which):
        width = src.shape[1]
        mine = at(group * width, width, 128)
        dst[:, mine] = src[...]

        @pl.loop(1, GROUP)
        def _(d):
            pltpu.make_async_remote_copy(
                src_ref=src,
                dst_ref=dst.at[:, mine],
                send_sem=small_tx.at[which],
                recv_sem=small_rx.at[which],
                device_id={"group": (group + d) % GROUP},
                device_id_type=MESH,
            ).start()

    def rep_gather(src, dst, which):
        mine = at(rep * 8, 8, 8)
        dst[mine, :] = src[...]

        @pl.loop(1, REP)
        def _(d):
            pltpu.make_async_remote_copy(
                src_ref=src,
                dst_ref=dst.at[mine, :],
                send_sem=small_tx.at[which],
                recv_sem=small_rx.at[which],
                device_id={"replica": (rep + d) % REP},
                device_id_type=MESH,
            ).start()

    def await_bytes(ref, sem):
        pltpu.make_async_copy(ref, ref, sem).wait()

    def after_rep_scatter(src, dst, total, which):
        await_bytes(dst, small_rx.at[which])
        value = src[at(rep * 8, 8, 8), :]
        for d in range(REP - 1):
            value = value + dst[d]
        total[...] = value

    def after_group_scatter(src, dst, total, which):
        await_bytes(dst, small_rx.at[which])
        width = src.shape[1] // GROUP
        value = src[:, at(group * width, width, 128)]
        for d in range(GROUP - 1):
            value = value + dst[d]
        total[...] = value

    def after_group_gather(dst, width, which):
        await_bytes(dst.at[:, pl.ds(0, 15 * width)], small_rx.at[which])

    def after_rep_gather(dst, which):
        await_bytes(dst.at[pl.ds(0, 56), :], small_rx.at[which])

    def place(i):
        k, j = i // 4, i % 4
        df = jnp.where(j == 0, 2, jnp.where(j == 1, 1, jnp.where(j == 2, 3, 0)))
        ds = jnp.where(k == 0, 2, jnp.where(k == 1, 1, jnp.where(k == 2, 3, 0)))
        return (
            at(ROWS * member(df, ds), 128, 128),
            at(ROWS * member(ds, df) + 128, 128, 128),
        )

    def project():
        q_l, q_r = split3(qt_ref[:, :FF]), split3(qt_ref[:, FF:])
        w_l = split3(fold3(dot_nn(q_l, ut[:FF, :])))
        w_r = split3(fold3(dot_nn(q_r, ut[FF:, :])))

        @pl.loop(0, GROUP)
        def _(i):
            p_l = fold3(dot_nn(w_l, xs[i])) * (1.0 / 128)
            p_r = fold3(dot_nn(w_r, gs[i])) * (1.0 / 128)
            low, high = place(i)
            pt[:RANK, low] = p_l[:, :128]
            pt[:RANK, high] = p_l[:, 128:]
            pt[RANK:, low] = p_r[:, :128]
            pt[RANK:, high] = p_r[:, 128:]

        mine = at(ROWS * group, ROWS, 128)
        for rows, columns, q3 in (
            (slice(0, RANK), slice(0, FF), q_l),
            (slice(RANK, 64), slice(FF, W), q_r),
        ):
            hi, low = split2(fb[:, columns])
            term = fold3(dot_nt(q3, hi)) + fold3(dot_nt(q3, low))
            pt[rows, mine] += term * (1.0 / 8)

    def back_project():
        def tile(i, state):
            y_l, y_r = state
            low, high = place(i)
            p = jnp.concatenate([pall[:, low], pall[:, high]], axis=1)
            return y_l + dot_nt(split3(p[:RANK]), xs[i]), y_r + dot_nt(split3(p[RANK:]), gs[i])

        zero = jnp.zeros((96, TOK), F32)
        y_l, y_r = lax.fori_loop(0, GROUP, tile, (zero, zero))
        y_l = split3(fold3(y_l) * (1.0 / 128))
        y_r = split3(fold3(y_r) * (1.0 / 128))
        p = pall[:, at(ROWS * group, ROWS, 128)] * (1.0 / 8)
        p_l, p_r = split3(p[:RANK]), split3(p[RANK:])

        def piece(y, p3, columns):
            hi, low = split2(fb[:, columns])
            return fold3(dot_nt(y, ut[columns, :])) + (fold3(dot_nn(p3, hi)) + fold3(dot_nn(p3, low)))

        for t in range(3):
            columns = slice(384 * t, 384 * t + 384)
            bt[:RANK, columns] = piece(y_l, p_l, columns)
        bt[RANK:, 0:640] = piece(y_l, p_l, slice(HALF, FF))
        bt[RANK:, 640:HALF] = piece(y_r, p_r, slice(FF, W))
        bt[:, HALF:] = jnp.zeros((64, BLEN - HALF), F32)

    def factors():
        gram_l = dot_nt_full(pall[:RANK, :], pall[:RANK, :])
        gram_r = dot_nt_full(pall[RANK:, :], pall[RANK:, :])
        return inverse_factor((gram_l, gram_r))

    def quad(v, last):
        hi, low = split2(v)
        return jnp.concatenate([hi, hi, low, low] if last else [hi, low, hi, low], axis=0)

    def bases(t_l, t_r, lanes):
        return jnp.concatenate(
            [
                quad(dot_nn_full(t_l, pall[:RANK, lanes]), True),
                quad(dot_nn_full(t_r, pall[RANK:, lanes]), True),
            ],
            axis=0,
        )

    def decompress(t_l, t_r):
        mine = bases(t_l, t_r, at(ROWS * group, ROWS, 128)).T
        pieces = (
            (t_l, slice(0, RANK), 0, 384, 0),
            (t_l, slice(0, RANK), 384, 768, 0),
            (t_l, slice(0, RANK), 768, 1152, 0),
            (t_l, slice(RANK, 64), 0, 640, HALF),
            (t_r, slice(RANK, 64), 640, HALF, HALF),
        )
        for t, rows, lo, hi, base in pieces:
            b4 = quad(dot_nn_full(t, ball[rows, lo:hi]), False)
            none = jnp.zeros_like(b4)
            left = base + lo < FF
            both = jnp.concatenate([b4, none] if left else [none, b4], axis=0)
            fb[:, base + lo : base + hi] -= dot_nn(mine, both)
            bk4[base + lo : base + hi, :] = both.T
        width = W // REP
        chosen = bk4[at(rep * width, width, 16), :]

        @pl.loop(0, 8)
        def _(t):
            basis = bases(t_l, t_r, at(t * 512, 512, 128)).T
            uout[at(t * 512, 512, 128), :] = dot_nt(basis, chosen).astype(BF16)

        pltpu.make_async_copy(uout, upd_hbm, out_sem.at[0]).start()

    pl.semaphore_wait(barrier, GROUP - 1 + REP - 1)

    opposite(0)
    pure(0)
    own(0)
    for i in range(4, GROUP):
        wait_step(i)
    pltpu.make_async_copy(fb_hbm, fb, load_fb).wait()
    project()
    rep_scatter(pt, prx, 0)
    opposite(1)
    dependent(0)
    pure(1)
    after_rep_scatter(pt, prx, psum, 0)
    group_scatter(psum, prx2, 1)
    complete(0)
    own(1)
    after_group_scatter(psum, prx2, psl, 1)
    group_gather(psl, pg, 2)
    opposite(2)
    dependent(1)
    after_group_gather(pg, ROWS, 2)
    rep_gather(pg, pall, 3)
    pure(2)
    complete(1)
    own(2)
    opposite(3)
    dependent(2)
    after_rep_gather(pall, 3)
    back_project()
    rep_scatter(bt, brx, 4)
    pure(3)
    complete(2)
    own(3)
    after_rep_scatter(bt, brx, bsum, 4)
    group_scatter(bsum, brx2, 5)
    dependent(3)
    t_l, t_r = factors()
    after_group_scatter(bsum, brx2, bsl, 5)
    group_gather(bsl, bg, 6)
    after_group_gather(bg, BLEN // GROUP, 6)
    rep_gather(bg, ball, 7)
    after_rep_gather(ball, 7)
    decompress(t_l, t_r)
    complete(3)

    for t in range(9):
        columns = slice(256 * t, 256 * t + 256)
        fb[:, columns] += pown[columns, :].T * (1.0 / GROUP)
    pltpu.make_async_copy(fb, new_hbm, out_sem.at[1]).start()

    for slot in pending:
        for c in copies(pending[slot]):
            c.wait_send()
    for which, ref in ((0, prx), (4, brx), (1, prx2), (5, brx2)):
        await_bytes(ref, small_tx.at[which])
    await_bytes(pg.at[:, pl.ds(0, 15 * ROWS)], small_tx.at[2])
    await_bytes(bg.at[:, pl.ds(0, 15 * (BLEN // GROUP))], small_tx.at[6])
    await_bytes(pall.at[pl.ds(0, 56), :], small_tx.at[3])
    await_bytes(ball.at[pl.ds(0, 56), :], small_tx.at[7])
    pltpu.make_async_copy(uout, upd_hbm, out_sem.at[0]).wait()
    pltpu.make_async_copy(fb, new_hbm, out_sem.at[1]).wait()


def on_device(layer_input, up_cotangent, attn_values, resid_cotangent, feedback, start_seed):
    factor = jnp.concatenate(
        [make_factor_t(start_seed, FF, 0), make_factor_t(start_seed, HD, 1)], axis=1
    )
    hbm = pl.BlockSpec(memory_space=pl.ANY)
    dma = pltpu.SemaphoreType.DMA
    new_feedback, update = pl.pallas_call(
        kernel,
        out_shape=(
            jax.ShapeDtypeStruct((ROWS, W), F32),
            jax.ShapeDtypeStruct((D, W // REP), BF16),
        ),
        in_specs=[hbm] * 5 + [pl.BlockSpec(memory_space=pltpu.VMEM)],
        out_specs=(hbm, hbm),
        scratch_shapes=[
            pltpu.VMEM((GROUP, TOK, ROWS), BF16),
            pltpu.VMEM((GROUP, TOK, ROWS), BF16),
            pltpu.VMEM((W, TOK), BF16),
            pltpu.VMEM((2, TOK, 256), BF16),
            pltpu.VMEM((HALF, ROWS), F32),
            pltpu.VMEM((W, ROWS), F32),
            pltpu.VMEM((W, ROWS), F32),
            pltpu.VMEM((14, HALF + 16, ROWS), jnp.int16),
            pltpu.VMEM((30, HALF + 16, ROWS), jnp.int16),
            pltpu.VMEM((ROWS, W), F32),
            pltpu.VMEM((64, D), F32),
            pltpu.VMEM((REP - 1, 8, D), F32),
            pltpu.VMEM((8, D), F32),
            pltpu.VMEM((GROUP - 1, 8, ROWS), F32),
            pltpu.VMEM((8, ROWS), F32),
            pltpu.VMEM((8, D), F32),
            pltpu.VMEM((64, D), F32),
            pltpu.VMEM((64, BLEN), F32),
            pltpu.VMEM((REP - 1, 8, BLEN), F32),
            pltpu.VMEM((8, BLEN), F32),
            pltpu.VMEM((GROUP - 1, 8, BLEN // GROUP), F32),
            pltpu.VMEM((8, BLEN // GROUP), F32),
            pltpu.VMEM((8, BLEN), F32),
            pltpu.VMEM((64, BLEN), F32),
            pltpu.VMEM((W, 256), BF16),
            pltpu.VMEM((D, W // REP), BF16),
            dma((GROUP,)),
            dma((GROUP,)),
            dma((2,)),
            dma,
            dma((2,)),
            dma((30, 2)),
            dma((30, 2)),
            dma((8,)),
            dma((8,)),
        ],
        compiler_params=pltpu.CompilerParams(
            collective_id=0, has_side_effects=True, vmem_limit_bytes=64 * 1024 * 1024 - 256 * 1024
        ),
        cost_estimate=pl.CostEstimate(flops=2 * TOK * D * W, bytes_accessed=21_000_000, transcendentals=0),
    )(layer_input, up_cotangent, attn_values, resid_cotangent, feedback[0], factor)
    return (update, new_feedback[None])


def solution(mesh):
    in_specs = (
        P(("replica", "group"), None),
        P(("replica", "group"), None),
        P(("replica", "group"), None),
        P(("replica", "group"), None),
        P("replica", "group", None),
        P(),
    )
    out_specs = (P(None, "replica"), P("replica", "group", None))
    return jax.shard_map(
        on_device, mesh=mesh, in_specs=in_specs, out_specs=out_specs, check_vma=False
    )
```

time: 654 us -> 159 us (0.24)
  waiting for transfers between devices: 461 us -> 0 us
  Pallas kernels: 0 us -> 148 us
  blocking collectives: 74.5 us -> 0 us
  other arithmetic: 46.2 us -> 1.69 us
  matrix products: 44.4 us -> 0 us
  between operations: 14.7 us -> 1.33 us
    reduce_scatter x1 -> x0, waiting for transfers between devices: 215 us -> none  [on_device(): lax.psum_scatter(jnp.concatenate([first, second], axis=1), 'group', scatt...]
    psum x3 -> x0, waiting for transfers between devices: 204 us -> none  [the longest x1 81 us: on_device(): lax.psum((highest(left_block.T, basis_left), highest(right_block.T, basis...]
    pallas_call x0 -> x1, Pallas kernels: none -> 148 us  [on_device(): pl.pallas_call(kernel, out_shape=(jax.ShapeDtypeStruct((ROWS, W), F32), j...]
    psum x1 -> x0, blocking collectives: 74.5 us -> none  [on_device(): lax.psum((highest(mean_left.T, mean_left), highest(mean_right.T, mean_rig...]
    dot_general x10 -> x0, matrix products: 42.4 us -> none  [the longest x1 19.9 us: on_device(): jnp.einsum('td,tf->df', layer_input, up_cotangent, preferred_element_type...]
    all_gather x1 -> x0, waiting for transfers between devices: 42.1 us -> none  [on_device(): update = lax.all_gather(piece, 'group', axis=0, tiled=True)]
    concatenate x1, other arithmetic: 26.1 us -> 0.73 us  [on_device(): jnp.concatenate([make_factor_t(start_seed, FF, 0), make_factor_t(start_se...]
    another operation x10 -> x0, other arithmetic: 13.4 us -> none  [the longest x4 6.22 us: solve_lower(): return jax.scipy.linalg.solve_triangular(lower, target.T, lower=True).T]
  transfers between devices with their start and end apart: 5 -> 0, of which waited for: 5 -> 0; matrix products, arithmetic and copies ran while one was open for 1% -> 0% of each run, Pallas kernels for 0% -> 0%
where the time goes in v1:
time: 159 us; the launch traced here: 157 us
  Pallas kernels  148 us (93%)
  local copies, waits for them, and re-layouts  6.01 us (4%)
  other arithmetic  1.69 us (1%)
    pallas_call x1, Pallas kernels, on_device(): pl.pallas_call(kernel, out_shape=(jax.ShapeDtypeStruct((ROWS, W), F32), j...  148 us
    unnamed x4, local copies, waits for them, and re-layouts  6.01 us

profile of v1, /device:TPU:0, one launch (start us, length us, event | category | flops | bytes accessed | tf_op | source)
XLA Modules:
  0.0 157.1 jit_solution(18184902791331252279)
XLA Ops:
  1.3 0.3 fusion.25
  1.6 0.7 fusion.8
  2.3 0.7 pad_maximum_fusion.qt_ref
  3.0 148.1 %shard_map.77 = (f32[256,2304]{1,0:T(8,128)}, bf16[4096,288]{1,0:T(8,128)(2,1)}) custom-call(bf16[768,4096]{1,0:T(8,128)(2,1)} %x_hbm.1, bf16[768,1792]{1,0:T(8,128)(2,1)} %u_hbm.1, bf16[768,512]{1,0:T(8,128)(2,1)} %a_hbm.1, bf16[768,4096]{1,0:T(8,128)(2,1)} %g_hbm.1, f32[256,2304]{1,0:T(8,128)} %bitcast.4, f32[32,2304]{1,0:T(8,128)} %pad_maximum_fusion.qt_ref), custom_call_target="tpu_custom_call" | custom-call | flops 14495514624 | bytes 21000000 | tf_op jit(solution)/shard_map/pallas_call | solution.py:549
  151.1 0.0 copy-start
  151.1 4.6 %copy.8 = bf16[4096,288]{0,1:T(8,128)(2,1)} copy(bf16[4096,288]{1,0:T(8,128)(2,1)} %get-tuple-element.6) | data formatting | bytes 4718592
  155.7 0.0 copy-done
  155.7 1.4 copy.11
  (3 shorter events, 0.0 us)
Async XLA Ops:
  151.1 4.6 %copy-start = (f32[256,2304]{1,0:T(8,128)S(1)}, f32[256,2304]{1,0:T(8,128)}, u32[]{:S(2)}) copy-start(f32[256,2304]{1,0:T(8,128)} %get-tuple-element.5) | copy-start | bytes 7077892

commit v2 on v1

v2 whole, which is shorter than its diff:
```python
import jax
import jax.numpy as jnp
from jax import lax
from jax.experimental import pallas as pl
from jax.experimental.pallas import tpu as pltpu
from jax.sharding import PartitionSpec as P

RANK = 32
TOK = 768
D = 4096
FF = 1792
HD = 512
W = FF + HD
HALF = W // 2
ROWS = 256
SIDE = 4
GROUP = 16
REP = 8
BLEN = 1536
LEVELS = 32700.0
ORDER = (2, 1, 3, 0)
MESH = pl.DeviceIdType.MESH
F32 = jnp.float32
BF16 = jnp.bfloat16
OPP_A, OPP_B, PURE_B, PURE_A, DEP_A, DEP_B = range(6)
RIGHTWARD = (True, False, True, False, True, False)


def modulo(v):
    r = v - jnp.floor(v * (1.0 / 65521.0)) * 65521.0
    r = jnp.where(r < 0.0, r + 65521.0, r)
    return jnp.where(r >= 65521.0, r - 65521.0, r)


def factor_t(seed, first, count, layer):
    positions = lax.broadcasted_iota(jnp.int32, (RANK, count), 1) + first
    columns = lax.broadcasted_iota(jnp.int32, (RANK, count), 0)
    base = (seed % 65521) * 31 + layer * 4099 + 12345
    mixed = modulo((base + positions * 977 + columns * 7919).astype(F32)).astype(jnp.int32)
    folded = (mixed & 255) * (mixed >> 8)
    final = modulo((folded * 181 + mixed).astype(F32))
    return (final / 65521.0 - 0.5) * 3.4


def split3(v):
    hi = v.astype(BF16)
    rest = v - hi.astype(F32)
    mid = rest.astype(BF16)
    low = (rest - mid.astype(F32)).astype(BF16)
    return jnp.concatenate([hi, mid, low], axis=0)


def split2(v):
    hi = v.astype(BF16)
    return hi, (v - hi.astype(F32)).astype(BF16)


def fold3(v):
    return (v[64:96] + v[32:64]) + v[0:32]


def dot_nn(a, b):
    return lax.dot_general(a, b, (((1,), (0,)), ((), ())), preferred_element_type=F32)


def dot_nt(a, b):
    return lax.dot_general(a, b, (((1,), (1,)), ((), ())), preferred_element_type=F32)


def dot_tn(a, b):
    return lax.dot_general(a, b, (((0,), (0,)), ((), ())), preferred_element_type=F32)


def dot_nt_full(a, b):
    return lax.dot_general(
        a, b, (((1,), (1,)), ((), ())), precision=lax.Precision.HIGHEST, preferred_element_type=F32
    )


def peak8(v):
    return jnp.max(jnp.abs(v).reshape(v.shape[0] // 8, 8, v.shape[1]), axis=0)


def at(start, size, step):
    return pl.ds(pl.multiple_of(start, step), size)


def pieces3(v):
    hi = v.astype(BF16)
    rest = v - hi.astype(F32)
    mid = rest.astype(BF16)
    return hi, mid, (rest - mid.astype(F32)).astype(BF16)


def apply_factor(t_t, v):
    hi, mid, low = pieces3(t_t)
    left = jnp.concatenate([hi, hi, hi, mid, mid, low], axis=0)
    hi, mid, low = pieces3(v)
    return dot_tn(left, jnp.concatenate([hi, mid, low, hi, mid, hi], axis=0))


def inverse_factor(gram):
    row = lax.broadcasted_iota(jnp.int32, (RANK, RANK), 0)
    lane = lax.broadcasted_iota(jnp.int32, (RANK, RANK), 1)
    eye = jnp.where(row == lane, 1.0, 0.0).astype(F32)

    def step(j, state):
        out = []
        for a, b in state:
            a_row = jnp.sum(jnp.where(row == j, a, 0.0), axis=0, keepdims=True)
            pivot = jnp.sum(jnp.where(lane[:1] == j, a_row, 0.0), axis=1, keepdims=True)
            a_col = jnp.sum(jnp.where(lane == j, a, 0.0), axis=1, keepdims=True)
            b_col = jnp.sum(jnp.where(lane == j, b, 0.0), axis=1, keepdims=True)
            factor = jnp.where(lane[:1] > j, a_row / pivot, 0.0)
            out.append((a - a_col * factor, b - b_col * factor))
        return tuple(out)

    state = lax.fori_loop(0, RANK, step, tuple((g, eye) for g in gram))
    result = []
    for a, b in state:
        diag = jnp.sum(jnp.where(row == lane, a, 0.0), axis=0, keepdims=True)
        result.append(b * (1.0 / jnp.sqrt(diag)))
    return result


def kernel(
    x_hbm, u_hbm, a_hbm, g_hbm, fb_hbm, seed_ref,
    new_hbm, upd_hbm,
    xs, gs, ut, ustg, tmp, pdep, pown, tx, rx, fb, q3,
    pt, pc, ps, py, pz, px, pall,
    bt, bc, bs, by, bz, bx, ball, bk4, uout,
    load_x, load_g, load_u, load_fb, out_sem,
    tx_sem, rx_sem, small_tx, small_rx,
):
    group = lax.axis_index("group")
    rep = lax.axis_index("replica")
    gx = group // SIDE
    gz = group % SIDE
    ry = rep // 2
    rc = rep % 2

    def member(dx, dz):
        return (gx + dx) % SIDE * SIDE + (gz + dz) % SIDE

    def replica(dy, dc):
        return (ry + dy) % SIDE * 2 + (rc + dc) % 2

    def load_step(k, j):
        df, ds = ORDER[j], ORDER[k]
        low = at(ROWS * member(df, ds), 128, 128)
        high = at(ROWS * member(ds, df) + 128, 128, 128)
        for src, dst, sem in ((x_hbm, xs, load_x), (g_hbm, gs, load_g)):
            for part, lanes in enumerate((low, high)):
                pltpu.make_async_copy(
                    src.at[:, lanes], dst.at[k, :, pl.ds(256 * j + 128 * part, 128)], sem.at[4 * k + j]
                ).start()

    load_a = pltpu.make_async_copy(u_hbm.at[:, pl.ds(0, HALF)], ustg, load_u.at[0])
    load_b = pltpu.make_async_copy(
        u_hbm.at[:, pl.ds(HALF, FF - HALF)], ustg.at[:, pl.ds(0, FF - HALF)], load_u.at[1]
    )
    load_c = pltpu.make_async_copy(a_hbm, ustg.at[:, pl.ds(FF - HALF, HD)], load_u.at[2])
    load_a.start()
    for k in range(SIDE):
        for j in range(SIDE):
            load_step(k, j)
    pltpu.make_async_copy(fb_hbm, fb, load_fb).start()
    loaded = set()

    def wait_step(k, j):
        if (k, j) in loaded:
            return
        loaded.add((k, j))
        for ref, sem in ((xs, load_x), (gs, load_g)):
            part = ref.at[k, :, pl.ds(256 * j, 256)]
            pltpu.make_async_copy(part, part, sem.at[4 * k + j]).wait()

    barrier = pltpu.get_barrier_semaphore()

    def greet(dy, dc, dx, dz):
        pl.semaphore_signal(
            barrier,
            inc=1,
            device_id={"replica": replica(dy, dc), "group": member(dx, dz)},
            device_id_type=MESH,
        )

    greet(0, 1, 0, 0)
    for d in range(1, SIDE):
        greet(d, 0, 0, 0)
        greet(1, 0, 0, d)
        greet(SIDE - 1, 0, 0, d)
        greet(0, 0, d, 0)
    greet(0, 0, 0, 1)
    greet(0, 0, 0, SIDE - 1)

    def transpose_u(base, sizes):
        start = 0
        for size in sizes:
            ut[base + start : base + start + size, :] = ustg[:, start : start + size].T
            start += size

    A_TILES = ((0, HALF, xs),)
    B_TILES = ((HALF, FF - HALF, xs), (FF, HD, gs))

    def products(k, lanes, tiles):
        row = 0
        for start, size, source in tiles:
            yield row, size, dot_nn(ut[start : start + size, :], source[k, :, lanes])
            row += size

    def matmul(k, j, tiles, dst, base):
        peak = jnp.zeros((8, ROWS), F32)
        for row, size, value in products(k, slice(256 * j, 256 * j + 256), tiles):
            dst[base + row : base + row + size, :] = value
            peak = jnp.maximum(peak, peak8(value))
        return peak

    def matmul_pair(k, tiles, dst_1, base_1, dst_2, base_2):
        peak = jnp.zeros((8, 2 * ROWS), F32)
        for row, size, value in products(k, slice(256, 768), tiles):
            dst_1[base_1 + row : base_1 + row + size, :] = value[:, :ROWS]
            dst_2[base_2 + row : base_2 + row + size, :] = value[:, ROWS:]
            peak = jnp.maximum(peak, peak8(value))
        return peak[:, :ROWS], peak[:, ROWS:]

    def quantise(src, base, m, slot):
        peak = jnp.maximum(jnp.max(m, axis=0, keepdims=True), 1e-30)
        power = jnp.ceil(jnp.log2(peak))
        scale = jnp.exp2(-power) * LEVELS

        @pl.loop(0, HALF // 64)
        def _(t):
            v = src[at(base + t * 64, 64, 64), :] * scale
            tx[slot, at(t * 64, 64, 64), :] = jnp.round(v).astype(jnp.int32).astype(jnp.int16)

        tx[slot, HALF : HALF + 16, :] = jnp.broadcast_to(power, (16, ROWS)).astype(jnp.int32).astype(jnp.int16)

    def copy_of(slot, mid, kind, stage, h):
        lanes = pl.ds(128 * h, 128)
        along_x = (h == 0) == (stage == 0)
        step = 1 if RIGHTWARD[kind] else SIDE - 1
        peer = member(step, 0) if along_x else member(0, step)
        return pltpu.make_async_remote_copy(
            src_ref=tx.at[slot, :, lanes],
            dst_ref=rx.at[mid, :, lanes],
            send_sem=tx_sem.at[mid, h],
            recv_sem=rx_sem.at[mid, h],
            device_id={"group": peer},
            device_id_type=MESH,
        )

    def slot_of(mid):
        chunk, kind = divmod(mid, 6)
        if chunk == 4:
            return 8 + kind
        return kind + (6 if chunk % 2 and kind < 2 else 0)

    def copies(mid):
        chunk, kind = divmod(mid, 6)
        return [copy_of(slot_of(mid), mid, kind, chunk // 4, h) for h in range(2)]

    pending = {}

    def send(mid, src, base, m):
        slot = slot_of(mid)
        if slot in pending:
            for c in copies(pending[slot]):
                c.wait_send()
        quantise(src, base, m, slot)
        for c in copies(mid):
            c.start()
        pending[slot] = mid

    def combine(acc, base, mids):
        for mid in mids:
            for c in copies(mid):
                c.wait_recv()
        scales = [
            jnp.exp2(rx[mid, HALF : HALF + 16, :].astype(jnp.int32).astype(F32)[:8]) * (1.0 / LEVELS)
            for mid in mids
        ]

        def tile(t, m):
            v = acc[at(base + t * 64, 64, 64), :].reshape(8, 8, ROWS)
            for mid, scale in zip(mids, scales):
                got = rx[mid, at(t * 64, 64, 64), :].astype(jnp.int32).astype(F32).reshape(8, 8, ROWS)
                v = v + got * scale[None]
            acc[at(base + t * 64, 64, 64), :] = v.reshape(64, ROWS)
            return jnp.maximum(m, jnp.max(jnp.abs(v), axis=0))

        return lax.fori_loop(0, HALF // 64, tile, jnp.zeros((8, ROWS), F32))

    def opposite_a(k):
        wait_step(k, 0)
        m = matmul(k, 0, A_TILES, tmp, 0)
        send(6 * k + OPP_A, tmp, 0, m)

    def opposite_b(k):
        m = matmul(k, 0, B_TILES, tmp, 0)
        send(6 * k + OPP_B, tmp, 0, m)

    def pure(k):
        wait_step(k, 1)
        wait_step(k, 2)
        m, _ = matmul_pair(k, B_TILES, tmp, 0, pdep, HALF)
        send(6 * k + PURE_B, tmp, 0, m)
        _, m = matmul_pair(k, A_TILES, pdep, 0, tmp, 0)
        send(6 * k + PURE_A, tmp, 0, m)

    def own(k):
        wait_step(k, 3)
        matmul(k, 3, A_TILES, pown, 0)
        matmul(k, 3, B_TILES, pown, HALF)

    def dependent(k):
        m = combine(pdep, 0, [6 * k + OPP_A])
        send(6 * k + DEP_A, pdep, 0, m)
        m = combine(pdep, HALF, [6 * k + OPP_B])
        send(6 * k + DEP_B, pdep, HALF, m)

    def complete(k):
        more_a = {0: [], 1: [24 + OPP_A], 2: [], 3: [24 + DEP_A, 24 + PURE_A]}[k]
        more_b = {0: [], 1: [], 2: [24 + OPP_B], 3: [24 + PURE_B, 24 + DEP_B]}[k]
        kind_a = {0: OPP_A, 1: DEP_A, 2: PURE_A}.get(k)
        kind_b = {0: OPP_B, 1: PURE_B, 2: DEP_B}.get(k)
        m = combine(pown, 0, [6 * k + DEP_A, 6 * k + PURE_A] + more_a)
        if k < 3:
            send(24 + kind_a, pown, 0, m)
        m = combine(pown, HALF, [6 * k + PURE_B, 6 * k + DEP_B] + more_b)
        if k < 3:
            send(24 + kind_b, pown, HALF, m)

    def post(src, dst, which, dy, dc, dx, dz):
        pltpu.make_async_remote_copy(
            src_ref=src,
            dst_ref=dst,
            send_sem=small_tx.at[which],
            recv_sem=small_rx.at[which],
            device_id={"replica": replica(dy, dc), "group": member(dx, dz)},
            device_id_type=MESH,
        ).start()

    def await_bytes(ref, sem):
        pltpu.make_async_copy(ref, ref, sem).wait()

    def all_reduce(src, core, total, chips, zs, xs_, result, first):
        length = src.shape[1]
        quarter = length // SIDE
        core_rows = at(rc * 32, 32, 32)
        my_rows = at(rc * 32 + ry * 8, 8, 8)

        def start():
            post(src.at[at((1 - rc) * 32, 32, 32), :], core, first, 0, 1, 0, 0)

        def along_y():
            await_bytes(core, small_rx.at[first])
            total[...] = src[core_rows, :] + core[...]
            for d in range(1, SIDE):
                post(total.at[at((ry + d) % SIDE * 8, 8, 8), :], chips.at[d - 1], first + 1, d, 0, 0, 0)

        def along_z():
            await_bytes(chips.at[pl.ds(0, 3)], small_rx.at[first + 1])
            chips[3] = (total[at(ry * 8, 8, 8), :] + chips[0]) + (chips[1] + chips[2])
            for d in range(SIDE):
                lanes = at((gz + d) % SIDE * quarter, quarter, 128)
                post(chips.at[3, :, lanes], zs.at[d], first + 2, 1, 0, 0, d)

        def along_x():
            await_bytes(zs.at[pl.ds(0, 4)], small_rx.at[first + 2])
            zs[4] = (zs[0] + zs[1]) + (zs[2] + zs[3])
            for d in range(1, SIDE):
                post(zs.at[4], xs_.at[gx], first + 3, 0, 0, d, 0)
            xs_[gx] = zs[4]

        def back_z():
            await_bytes(xs_.at[pl.ds(0, 3)], small_rx.at[first + 3])
            xs_[4] = (xs_[0] + xs_[1]) + (xs_[2] + xs_[3])
            rows = at(rc * 32 + (ry + SIDE - 1) % SIDE * 8, 8, 8)
            for d in range(SIDE):
                post(
                    xs_.at[4], result.at[rows, at(gz * quarter, quarter, 128)], first + 4, SIDE - 1, 0, 0, d
                )

        def back_y():
            await_bytes(result.at[pl.ds(0, 8), :], small_rx.at[first + 4])
            for d in range(1, SIDE):
                post(result.at[my_rows, :], result.at[my_rows, :], first + 5, d, 0, 0, 0)

        def back_core():
            await_bytes(result.at[pl.ds(0, 24), :], small_rx.at[first + 5])
            post(result.at[core_rows, :], result.at[core_rows, :], first + 6, 0, 1, 0, 0)

        def done():
            await_bytes(result.at[pl.ds(0, 32), :], small_rx.at[first + 6])

        def sent():
            await_bytes(result.at[pl.ds(0, 32), :], small_tx.at[first])
            await_bytes(result.at[pl.ds(0, 24), :], small_tx.at[first + 1])
            await_bytes(result.at[pl.ds(0, 8), :], small_tx.at[first + 2])
            await_bytes(xs_.at[pl.ds(0, 3)], small_tx.at[first + 3])
            await_bytes(result.at[pl.ds(0, 8), :], small_tx.at[first + 4])
            await_bytes(result.at[pl.ds(0, 24), :], small_tx.at[first + 5])
            await_bytes(result.at[pl.ds(0, 32), :], small_tx.at[first + 6])

        return start, along_y, along_z, along_x, back_z, back_y, back_core, done, sent

    def lanes_of(k, j):
        df, ds = ORDER[j], ORDER[k]
        return at(ROWS * member(df, ds), 128, 128), at(ROWS * member(ds, df) + 128, 128, 128)

    def make_factors():
        seed = seed_ref[0]
        for t in range(9):
            layer = t // 7
            q = factor_t(seed, 256 * (t - 7 * layer), 256, layer)
            q3[:, 256 * t : 256 * t + 256] = split3(q)

    def project():
        w_l = split3(fold3(dot_nn(q3[:, :FF], ut[:FF, :])))
        w_r = split3(fold3(dot_nn(q3[:, FF:], ut[FF:, :])))
        for k in range(SIDE):
            p_l = fold3(dot_nn(w_l, xs[k])) * (1.0 / 128)
            p_r = fold3(dot_nn(w_r, gs[k])) * (1.0 / 128)
            for j in range(SIDE):
                for part, lanes in enumerate(lanes_of(k, j)):
                    here = slice(256 * j + 128 * part, 256 * j + 128 * part + 128)
                    pt[:RANK, lanes] = p_l[:, here]
                    pt[RANK:, lanes] = p_r[:, here]

        mine = at(ROWS * group, ROWS, 128)
        for rows, columns in ((slice(0, RANK), slice(0, FF)), (slice(RANK, 64), slice(FF, W))):
            hi, low = split2(fb[:, columns])
            term = fold3(dot_nt(q3[:, columns], hi)) + fold3(dot_nt(q3[:, columns], low))
            pt[rows, mine] += term * (1.0 / 8)

    def back_project():
        y_l = jnp.zeros((96, TOK), F32)
        y_r = jnp.zeros((96, TOK), F32)
        for k in range(SIDE):
            parts = []
            for j in range(SIDE):
                for lanes in lanes_of(k, j):
                    parts.append(pall[:, lanes])
            p = jnp.concatenate(parts, axis=1)
            y_l = y_l + dot_nt(split3(p[:RANK]), xs[k])
            y_r = y_r + dot_nt(split3(p[RANK:]), gs[k])
        y_l = split3(fold3(y_l) * (1.0 / 128))
        y_r = split3(fold3(y_r) * (1.0 / 128))
        p = pall[:, at(ROWS * group, ROWS, 128)] * (1.0 / 8)
        p_l, p_r = split3(p[:RANK]), split3(p[RANK:])

        def piece(y, p3, columns):
            hi, low = split2(fb[:, columns])
            return fold3(dot_nt(y, ut[columns, :])) + (fold3(dot_nn(p3, hi)) + fold3(dot_nn(p3, low)))

        bt[:RANK, :HALF] = piece(y_l, p_l, slice(0, HALF))
        bt[RANK:, 0:640] = piece(y_l, p_l, slice(HALF, FF))
        bt[RANK:, 640:HALF] = piece(y_r, p_r, slice(FF, W))
        bt[:, HALF:] = jnp.zeros((64, BLEN - HALF), F32)

    def factors():
        gram_l = dot_nt_full(pall[:RANK, :], pall[:RANK, :])
        gram_r = dot_nt_full(pall[RANK:, :], pall[RANK:, :])
        return inverse_factor((gram_l, gram_r))

    def quad(v, last):
        hi, low = split2(v)
        return jnp.concatenate([hi, hi, low, low] if last else [hi, low, hi, low], axis=0)

    def bases(t_l, t_r, lanes):
        return jnp.concatenate(
            [
                quad(apply_factor(t_l, pall[:RANK, lanes]), True),
                quad(apply_factor(t_r, pall[RANK:, lanes]), True),
            ],
            axis=0,
        )

    def decompress(t_l, t_r):
        mine = bases(t_l, t_r, at(ROWS * group, ROWS, 128)).T
        pieces = (
            (t_l, slice(0, RANK), 0, HALF, 0),
            (t_l, slice(RANK, 64), 0, 640, HALF),
            (t_r, slice(RANK, 64), 640, HALF, HALF),
        )
        for t, rows, lo, hi, base in pieces:
            b4 = quad(apply_factor(t, ball[rows, lo:hi]), False)
            none = jnp.zeros_like(b4)
            left = base + lo < FF
            both = jnp.concatenate([b4, none] if left else [none, b4], axis=0)
            fb[:, base + lo : base + hi] -= dot_nn(mine, both)
            bk4[base + lo : base + hi, :] = both.T
        width = W // REP
        chosen = bk4[at(rep * width, width, 16), :]
        for t in range(4):
            lanes = slice(1024 * t, 1024 * t + 1024)
            uout[:, lanes] = dot_nn(chosen, bases(t_l, t_r, lanes)).astype(BF16)
        pltpu.make_async_copy(uout, upd_hbm, out_sem.at[0]).start()

    p_steps = all_reduce(pt, pc, ps, py, pz, px, pall, 0)
    b_steps = all_reduce(bt, bc, bs, by, bz, bx, ball, 7)

    load_a.wait()
    transpose_u(0, (384, 384, 384))
    load_b.start()
    load_c.start()
    pl.semaphore_wait(barrier, 15)
    opposite_a(0)
    load_b.wait()
    load_c.wait()
    transpose_u(HALF, (256, 384, 256, 256))
    opposite_b(0)
    pure(0)
    make_factors()
    for k in range(SIDE):
        for j in range(SIDE):
            wait_step(k, j)
    pltpu.make_async_copy(fb_hbm, fb, load_fb).wait()
    project()
    p_steps[0]()
    own(0)
    p_steps[1]()
    opposite_a(1)
    opposite_b(1)
    dependent(0)
    pure(1)
    p_steps[2]()
    dependent(1)
    p_steps[3]()
    complete(0)
    opposite_a(2)
    opposite_b(2)
    own(1)
    p_steps[4]()
    pure(2)
    p_steps[5]()
    dependent(2)
    p_steps[6]()
    complete(1)
    p_steps[7]()
    back_project()
    b_steps[0]()
    own(2)
    b_steps[1]()
    opposite_a(3)
    opposite_b(3)
    b_steps[2]()
    pure(3)
    b_steps[3]()
    dependent(3)
    t_l, t_r = factors()
    complete(2)
    b_steps[4]()
    own(3)
    b_steps[5]()
    b_steps[6]()
    b_steps[7]()
    decompress(t_l, t_r)
    complete(3)

    for t in range(9):
        columns = slice(256 * t, 256 * t + 256)
        fb[:, columns] += pown[columns, :].T * (1.0 / GROUP)
    pltpu.make_async_copy(fb, new_hbm, out_sem.at[1]).start()

    for slot in pending:
        for c in copies(pending[slot]):
            c.wait_send()
    p_steps[8]()
    b_steps[8]()
    pltpu.make_async_copy(uout, upd_hbm, out_sem.at[0]).wait()
    pltpu.make_async_copy(fb, new_hbm, out_sem.at[1]).wait()


def small_buffers(length):
    quarter = length // SIDE
    shapes = (
        (64, length), (32, length), (32, length), (4, 8, length), (5, 8, quarter), (5, 8, quarter), (64, length)
    )
    return [pltpu.VMEM(shape, F32) for shape in shapes]


def on_device(layer_input, up_cotangent, attn_values, resid_cotangent, feedback, start_seed):
    hbm = pl.BlockSpec(memory_space=pl.ANY)
    dma = pltpu.SemaphoreType.DMA
    new_feedback, update = pl.pallas_call(
        kernel,
        out_shape=(
            jax.ShapeDtypeStruct((ROWS, W), F32),
            jax.ShapeDtypeStruct((W // REP, D), BF16),
        ),
        in_specs=[hbm] * 5 + [pl.BlockSpec(memory_space=pltpu.SMEM)],
        out_specs=(hbm, hbm),
        scratch_shapes=[
            pltpu.VMEM((SIDE, TOK, SIDE * ROWS), BF16),
            pltpu.VMEM((SIDE, TOK, SIDE * ROWS), BF16),
            pltpu.VMEM((W, TOK), BF16),
            pltpu.VMEM((TOK, HALF), BF16),
            pltpu.VMEM((HALF, ROWS), F32),
            pltpu.VMEM((W, ROWS), F32),
            pltpu.VMEM((W, ROWS), F32),
            pltpu.VMEM((14, HALF + 16, ROWS), jnp.int16),
            pltpu.VMEM((30, HALF + 16, ROWS), jnp.int16),
            pltpu.VMEM((ROWS, W), F32),
            pltpu.VMEM((96, W), BF16),
            *small_buffers(D),
            *small_buffers(BLEN),
            pltpu.VMEM((W, 256), BF16),
            pltpu.VMEM((W // REP, D), BF16),
            dma((GROUP,)),
            dma((GROUP,)),
            dma((3,)),
            dma,
            dma((2,)),
            dma((30, 2)),
            dma((30, 2)),
            dma((14,)),
            dma((14,)),
        ],
        compiler_params=pltpu.CompilerParams(
            collective_id=0, has_side_effects=True, vmem_limit_bytes=64 * 1024 * 1024 - 256 * 1024
        ),
        cost_estimate=pl.CostEstimate(flops=2 * TOK * D * W, bytes_accessed=21_000_000, transcendentals=0),
    )(layer_input, up_cotangent, attn_values, resid_cotangent, feedback[0], start_seed)
    return (update.T, new_feedback[None])


def solution(mesh):
    in_specs = (
        P(("replica", "group"), None),
        P(("replica", "group"), None),
        P(("replica", "group"), None),
        P(("replica", "group"), None),
        P("replica", "group", None),
        P(),
    )
    out_specs = (P(None, "replica"), P("replica", "group", None))
    return jax.shard_map(
        on_device, mesh=mesh, in_specs=in_specs, out_specs=out_specs, check_vma=False
    )
```

time: 159 us -> 133 us (0.84)
  Pallas kernels: 148 us -> 125 us
  other arithmetic: 1.69 us -> 0 us
    pallas_call x1, Pallas kernels: 148 us -> 125 us  [on_device(): pl.pallas_call(kernel, out_shape=(jax.ShapeDtypeStruct((ROWS, W), F32), j...]
where the time goes in v2:
time: 133 us; the launch traced here: 131 us
  Pallas kernels  125 us (94%)
  local copies, waits for them, and re-layouts  4.88 us (4%)
    pallas_call x1, Pallas kernels, on_device(): pl.pallas_call(kernel, out_shape=(jax.ShapeDtypeStruct((ROWS, W), F32), j...  125 us
    unnamed x4, local copies, waits for them, and re-layouts  4.88 us

profile of v2, /device:TPU:0, one launch (start us, length us, event | category | flops | bytes accessed | tf_op | source)
XLA Modules:
  0.0 131.5 jit_solution(6686808179779196133)
XLA Ops:
  1.3 125.3 %shard_map.77 = (f32[256,2304]{1,0:T(8,128)}, bf16[288,4096]{1,0:T(8,128)(2,1)}) custom-call(bf16[768,4096]{1,0:T(8,128)(2,1)} %x_hbm.1, bf16[768,1792]{1,0:T(8,128)(2,1)} %u_hbm.1, bf16[768,512]{1,0:T(8,128)(2,1)} %a_hbm.1, bf16[768,4096]{1,0:T(8,128)(2,1)} %g_hbm.1, f32[256,2304]{1,0:T(8,128)} %bitcast.5, s32[1]{0:T(128)S(6)} %copy.10.seed_ref), custom_call_target="tpu_custom_call" | custom-call | flops 14495514624 | bytes 21000000 | tf_op jit(solution)/shard_map/pallas_call | solution.py:587
  126.6 0.0 copy-start
  126.6 3.5 %copy.11 = bf16[4096,288]{0,1:T(8,128)(2,1)} copy(bf16[4096,288]{0,1:T(8,128)(2,1)} %bitcast.4) | data formatting | bytes 4718592
  130.1 0.0 copy-done
  130.1 1.4 %copy.12 = f32[1,256,2304]{2,1,0:T(8,128)} copy(f32[1,256,2304]{2,1,0:T(8,128)S(1)} %bitcast.3) | data formatting | bytes 4718592
Async XLA Ops:
  126.6 3.5 %copy-start = (f32[256,2304]{1,0:T(8,128)S(1)}, f32[256,2304]{1,0:T(8,128)}, u32[]{:S(2)}) copy-start(f32[256,2304]{1,0:T(8,128)} %get-tuple-element.5) | copy-start | bytes 7077892

commit v3 on v2

--- a/solution.py
+++ b/solution.py
@@ -99,10 +99,9 @@
     return dot_tn(left, jnp.concatenate([hi, mid, low, hi, mid, hi], axis=0))
 
 
-def inverse_factor(gram):
+def eliminate(state, first, last):
     row = lax.broadcasted_iota(jnp.int32, (RANK, RANK), 0)
     lane = lax.broadcasted_iota(jnp.int32, (RANK, RANK), 1)
-    eye = jnp.where(row == lane, 1.0, 0.0).astype(F32)
 
     def step(j, state):
         out = []
@@ -115,12 +114,18 @@
             out.append((a - a_col * factor, b - b_col * factor))
         return tuple(out)
 
-    state = lax.fori_loop(0, RANK, step, tuple((g, eye) for g in gram))
-    result = []
-    for a, b in state:
-        diag = jnp.sum(jnp.where(row == lane, a, 0.0), axis=0, keepdims=True)
-        result.append(b * (1.0 / jnp.sqrt(diag)))
-    return result
+    return lax.fori_loop(first, last, step, state)
+
+
+def identity():
+    row = lax.broadcasted_iota(jnp.int32, (RANK, RANK), 0)
+    lane = lax.broadcasted_iota(jnp.int32, (RANK, RANK), 1)
+    return jnp.where(row == lane, 1.0, 0.0).astype(F32)
+
+
+def scaled(state):
+    eye = identity()
+    return [b * (1.0 / jnp.sqrt(jnp.sum(a * eye, axis=0, keepdims=True))) for a, b in state]
 
 
 def kernel(
@@ -262,15 +267,19 @@
 
     pending = {}
 
-    def send(mid, src, base, m):
+    def send(mid, src, base, m, held=()):
         slot = slot_of(mid)
         if slot in pending:
             for c in copies(pending[slot]):
                 c.wait_send()
         quantise(src, base, m, slot)
-        for c in copies(mid):
-            c.start()
+        for h, c in enumerate(copies(mid)):
+            if h not in held:
+                c.start()
         pending[slot] = mid
+
+    def release(mid, h):
+        copies(mid)[h].start()
 
     def combine(acc, base, mids):
         for mid in mids:
@@ -291,20 +300,25 @@
 
         return lax.fori_loop(0, HALF // 64, tile, jnp.zeros((8, ROWS), F32))
 
-    def opposite_a(k):
+    def opposite_a(k, held=()):
         wait_step(k, 0)
         m = matmul(k, 0, A_TILES, tmp, 0)
-        send(6 * k + OPP_A, tmp, 0, m)
+        send(6 * k + OPP_A, tmp, 0, m, held)
 
     def opposite_b(k):
+        wait_step(k, 0)
         m = matmul(k, 0, B_TILES, tmp, 0)
         send(6 * k + OPP_B, tmp, 0, m)
 
-    def pure(k):
+    def pure_b(k, held=()):
         wait_step(k, 1)
         wait_step(k, 2)
         m, _ = matmul_pair(k, B_TILES, tmp, 0, pdep, HALF)
-        send(6 * k + PURE_B, tmp, 0, m)
+        send(6 * k + PURE_B, tmp, 0, m, held)
+
+    def pure_a(k):
+        wait_step(k, 1)
+        wait_step(k, 2)
         _, m = matmul_pair(k, A_TILES, pdep, 0, tmp, 0)
         send(6 * k + PURE_A, tmp, 0, m)
 
@@ -313,23 +327,25 @@
         matmul(k, 3, A_TILES, pown, 0)
         matmul(k, 3, B_TILES, pown, HALF)
 
-    def dependent(k):
+    def dependent_a(k):
         m = combine(pdep, 0, [6 * k + OPP_A])
         send(6 * k + DEP_A, pdep, 0, m)
+
+    def dependent_b(k):
         m = combine(pdep, HALF, [6 * k + OPP_B])
         send(6 * k + DEP_B, pdep, HALF, m)
 
-    def complete(k):
-        more_a = {0: [], 1: [24 + OPP_A], 2: [], 3: [24 + DEP_A, 24 + PURE_A]}[k]
-        more_b = {0: [], 1: [], 2: [24 + OPP_B], 3: [24 + PURE_B, 24 + DEP_B]}[k]
-        kind_a = {0: OPP_A, 1: DEP_A, 2: PURE_A}.get(k)
-        kind_b = {0: OPP_B, 1: PURE_B, 2: DEP_B}.get(k)
-        m = combine(pown, 0, [6 * k + DEP_A, 6 * k + PURE_A] + more_a)
+    def complete_a(k):
+        more = {0: [], 1: [24 + OPP_A], 2: [], 3: [24 + DEP_A, 24 + PURE_A]}[k]
+        m = combine(pown, 0, [6 * k + DEP_A, 6 * k + PURE_A] + more)
         if k < 3:
-            send(24 + kind_a, pown, 0, m)
-        m = combine(pown, HALF, [6 * k + PURE_B, 6 * k + DEP_B] + more_b)
+            send(24 + (OPP_A, DEP_A, PURE_A)[k], pown, 0, m)
+
+    def complete_b(k):
+        more = {0: [], 1: [], 2: [24 + OPP_B], 3: [24 + PURE_B, 24 + DEP_B]}[k]
+        m = combine(pown, HALF, [6 * k + PURE_B, 6 * k + DEP_B] + more)
         if k < 3:
-            send(24 + kind_b, pown, HALF, m)
+            send(24 + (OPP_B, PURE_B, DEP_B)[k], pown, HALF, m)
 
     def post(src, dst, which, dy, dc, dx, dz):
         pltpu.make_async_remote_copy(
@@ -459,10 +475,11 @@
         bt[RANK:, 640:HALF] = piece(y_r, p_r, slice(FF, W))
         bt[:, HALF:] = jnp.zeros((64, BLEN - HALF), F32)
 
-    def factors():
-        gram_l = dot_nt_full(pall[:RANK, :], pall[:RANK, :])
-        gram_r = dot_nt_full(pall[RANK:, :], pall[RANK:, :])
-        return inverse_factor((gram_l, gram_r))
+    def grams():
+        eye = identity()
+        return tuple(
+            (dot_nt_full(pall[rows, :], pall[rows, :]), eye) for rows in (slice(0, RANK), slice(RANK, 64))
+        )
 
     def quad(v, last):
         hi, low = split2(v)
@@ -511,7 +528,8 @@
     load_c.wait()
     transpose_u(HALF, (256, 384, 256, 256))
     opposite_b(0)
-    pure(0)
+    pure_b(0)
+    pure_a(0)
     make_factors()
     for k in range(SIDE):
         for j in range(SIDE):
@@ -523,41 +541,57 @@
     p_steps[1]()
     opposite_a(1)
     opposite_b(1)
-    dependent(0)
-    pure(1)
+    dependent_a(0)
+    dependent_b(0)
+    pure_b(1)
+    pure_a(1)
     p_steps[2]()
-    dependent(1)
     p_steps[3]()
-    complete(0)
+    dependent_a(1)
+    dependent_b(1)
+    complete_a(0)
+    complete_b(0)
     opposite_a(2)
     opposite_b(2)
     own(1)
     p_steps[4]()
-    pure(2)
+    pure_b(2)
+    pure_a(2)
     p_steps[5]()
-    dependent(2)
+    dependent_a(2)
+    dependent_b(2)
     p_steps[6]()
-    complete(1)
+    complete_a(1)
+    complete_b(1)
     p_steps[7]()
     back_project()
     b_steps[0]()
+    opposite_b(3)
+    opposite_a(3, held=(0,))
+    b_steps[1]()
     own(2)
-    b_steps[1]()
-    opposite_a(3)
-    opposite_b(3)
+    pure_a(3)
+    pure_b(3, held=(0,))
+    state = eliminate(grams(), 0, 8)
     b_steps[2]()
-    pure(3)
+    state = eliminate(state, 8, 20)
     b_steps[3]()
-    dependent(3)
-    t_l, t_r = factors()
-    complete(2)
+    release(18 + OPP_A, 0)
+    release(18 + PURE_B, 0)
+    complete_b(2)
+    complete_a(2)
+    state = eliminate(state, 20, RANK)
+    t_l, t_r = scaled(state)
     b_steps[4]()
     own(3)
+    dependent_b(3)
     b_steps[5]()
     b_steps[6]()
+    dependent_a(3)
     b_steps[7]()
     decompress(t_l, t_r)
-    complete(3)
+    complete_b(3)
+    complete_a(3)
 
     for t in range(9):
         columns = slice(256 * t, 256 * t + 256)

time: 133 us -> 124 us (0.932)
  Pallas kernels: 125 us -> 118 us
    pallas_call x1, Pallas kernels: 125 us -> 118 us  [on_device(): pl.pallas_call(kernel, out_shape=(jax.ShapeDtypeStruct((ROWS, W), F32), j...]
where the time goes in v3:
time: 124 us
  Pallas kernels  118 us (95%)
  local copies, waits for them, and re-layouts  4.88 us (4%)
  between operations  1.3 us (1%)
    pallas_call x1, Pallas kernels, on_device(): pl.pallas_call(kernel, out_shape=(jax.ShapeDtypeStruct((ROWS, W), F32), j...  118 us
    unnamed x4, local copies, waits for them, and re-layouts  4.88 us

profile of v3, /device:TPU:0, one launch (start us, length us, event | category | flops | bytes accessed | tf_op | source)
XLA Modules:
  0.0 123.8 jit_solution(14471435560234216831)
XLA Ops:
  1.3 117.6 %shard_map.77 = (f32[256,2304]{1,0:T(8,128)}, bf16[288,4096]{1,0:T(8,128)(2,1)}) custom-call(bf16[768,4096]{1,0:T(8,128)(2,1)} %x_hbm.1, bf16[768,1792]{1,0:T(8,128)(2,1)} %u_hbm.1, bf16[768,512]{1,0:T(8,128)(2,1)} %a_hbm.1, bf16[768,4096]{1,0:T(8,128)(2,1)} %g_hbm.1, f32[256,2304]{1,0:T(8,128)} %bitcast.5, s32[1]{0:T(128)S(6)} %copy.10.seed_ref), custom_call_target="tpu_custom_call" | custom-call | flops 14495514624 | bytes 21000000 | tf_op jit(solution)/shard_map/pallas_call | solution.py:621
  118.9 0.0 copy-start
  118.9 3.5 %copy.11 = bf16[4096,288]{0,1:T(8,128)(2,1)} copy(bf16[4096,288]{0,1:T(8,128)(2,1)} %bitcast.4) | data formatting | bytes 4718592
  122.4 0.0 copy-done
  122.4 1.4 %copy.12 = f32[1,256,2304]{2,1,0:T(8,128)} copy(f32[1,256,2304]{2,1,0:T(8,128)S(1)} %bitcast.3) | data formatting | bytes 4718592
Async XLA Ops:
  118.9 3.5 %copy-start = (f32[256,2304]{1,0:T(8,128)S(1)}, f32[256,2304]{1,0:T(8,128)}, u32[]{:S(2)}) copy-start(f32[256,2304]{1,0:T(8,128)} %get-tuple-element.5) | copy-start | bytes 7077892

commit v4 on v3

--- a/solution.py
+++ b/solution.py
@@ -130,11 +130,11 @@
 
 def kernel(
     x_hbm, u_hbm, a_hbm, g_hbm, fb_hbm, seed_ref,
-    new_hbm, upd_hbm,
-    xs, gs, ut, ustg, tmp, pdep, pown, tx, rx, fb, q3,
+    fb, uout,
+    xs, gs, ut, ustg, tmp, pdep, pown, tx, rx, q3,
     pt, pc, ps, py, pz, px, pall,
-    bt, bc, bs, by, bz, bx, ball, bk4, uout,
-    load_x, load_g, load_u, load_fb, out_sem,
+    bt, bc, bs, by, bz, bx, ball, bk4,
+    load_x, load_g, load_u, load_fb,
     tx_sem, rx_sem, small_tx, small_rx,
 ):
     group = lax.axis_index("group")
@@ -165,11 +165,13 @@
         u_hbm.at[:, pl.ds(HALF, FF - HALF)], ustg.at[:, pl.ds(0, FF - HALF)], load_u.at[1]
     )
     load_c = pltpu.make_async_copy(a_hbm, ustg.at[:, pl.ds(FF - HALF, HD)], load_u.at[2])
-    load_a.start()
-    for k in range(SIDE):
-        for j in range(SIDE):
-            load_step(k, j)
-    pltpu.make_async_copy(fb_hbm, fb, load_fb).start()
+    def load_rest():
+        for k in range(SIDE):
+            for j in range(SIDE):
+                if k > 0 or j == SIDE - 1:
+                    load_step(k, j)
+        pltpu.make_async_copy(fb_hbm, fb, load_fb).start()
+
     loaded = set()
 
     def wait_step(k, j):
@@ -190,6 +192,8 @@
             device_id_type=MESH,
         )
 
+    load_a.start()
+    load_step(0, 0)
     greet(0, 1, 0, 0)
     for d in range(1, SIDE):
         greet(d, 0, 0, 0)
@@ -281,14 +285,15 @@
     def release(mid, h):
         copies(mid)[h].start()
 
+    def scale_of(mid):
+        power = rx[mid, HALF : HALF + 16, :].astype(jnp.int32).astype(F32)[:8]
+        return jnp.exp2(power) * (1.0 / LEVELS)
+
     def combine(acc, base, mids):
         for mid in mids:
             for c in copies(mid):
                 c.wait_recv()
-        scales = [
-            jnp.exp2(rx[mid, HALF : HALF + 16, :].astype(jnp.int32).astype(F32)[:8]) * (1.0 / LEVELS)
-            for mid in mids
-        ]
+        scales = [scale_of(mid) for mid in mids]
 
         def tile(t, m):
             v = acc[at(base + t * 64, 64, 64), :].reshape(8, 8, ROWS)
@@ -336,16 +341,28 @@
         send(6 * k + DEP_B, pdep, HALF, m)
 
     def complete_a(k):
-        more = {0: [], 1: [24 + OPP_A], 2: [], 3: [24 + DEP_A, 24 + PURE_A]}[k]
+        more = {0: [], 1: [24 + OPP_A], 2: []}[k]
         m = combine(pown, 0, [6 * k + DEP_A, 6 * k + PURE_A] + more)
-        if k < 3:
-            send(24 + (OPP_A, DEP_A, PURE_A)[k], pown, 0, m)
+        send(24 + (OPP_A, DEP_A, PURE_A)[k], pown, 0, m)
 
     def complete_b(k):
-        more = {0: [], 1: [], 2: [24 + OPP_B], 3: [24 + PURE_B, 24 + DEP_B]}[k]
+        more = {0: [], 1: [], 2: [24 + OPP_B]}[k]
         m = combine(pown, HALF, [6 * k + PURE_B, 6 * k + DEP_B] + more)
-        if k < 3:
-            send(24 + (OPP_B, PURE_B, DEP_B)[k], pown, HALF, m)
+        send(24 + (OPP_B, PURE_B, DEP_B)[k], pown, HALF, m)
+
+    def finish(base, mids, with_own):
+        for mid in mids:
+            for c in copies(mid):
+                c.wait_recv()
+        scales = [scale_of(mid) for mid in mids]
+        for t in range(HALF // 128):
+            rows = slice(128 * t, 128 * t + 128)
+            v = pown[base + 128 * t : base + 128 * t + 128, :].reshape(16, 8, ROWS) if with_own else None
+            for mid, scale in zip(mids, scales):
+                got = rx[mid, rows, :].astype(jnp.int32).astype(F32).reshape(16, 8, ROWS) * scale[None]
+                v = got if v is None else v + got
+            columns = slice(base + 128 * t, base + 128 * t + 128)
+            fb[:, columns] += v.reshape(128, ROWS).T * (1.0 / GROUP)
 
     def post(src, dst, which, dy, dc, dx, dz):
         pltpu.make_async_remote_copy(
@@ -508,16 +525,19 @@
             both = jnp.concatenate([b4, none] if left else [none, b4], axis=0)
             fb[:, base + lo : base + hi] -= dot_nn(mine, both)
             bk4[base + lo : base + hi, :] = both.T
+
+    def decompress_update(t_l, t_r):
         width = W // REP
         chosen = bk4[at(rep * width, width, 16), :]
         for t in range(4):
             lanes = slice(1024 * t, 1024 * t + 1024)
             uout[:, lanes] = dot_nn(chosen, bases(t_l, t_r, lanes)).astype(BF16)
-        pltpu.make_async_copy(uout, upd_hbm, out_sem.at[0]).start()
 
     p_steps = all_reduce(pt, pc, ps, py, pz, px, pall, 0)
     b_steps = all_reduce(bt, bc, bs, by, bz, bx, ball, 7)
 
+    load_step(0, 1)
+    load_step(0, 2)
     load_a.wait()
     transpose_u(0, (384, 384, 384))
     load_b.start()
@@ -527,6 +547,7 @@
     load_b.wait()
     load_c.wait()
     transpose_u(HALF, (256, 384, 256, 256))
+    load_rest()
     opposite_b(0)
     pure_b(0)
     pure_a(0)
@@ -588,23 +609,19 @@
     b_steps[5]()
     b_steps[6]()
     dependent_a(3)
+    finish(0, [18 + PURE_A, 24 + DEP_A, 24 + PURE_A], True)
+    finish(HALF, [18 + PURE_B, 24 + PURE_B, 24 + DEP_B], True)
     b_steps[7]()
     decompress(t_l, t_r)
-    complete_b(3)
-    complete_a(3)
-
-    for t in range(9):
-        columns = slice(256 * t, 256 * t + 256)
-        fb[:, columns] += pown[columns, :].T * (1.0 / GROUP)
-    pltpu.make_async_copy(fb, new_hbm, out_sem.at[1]).start()
+    decompress_update(t_l, t_r)
+    finish(HALF, [18 + DEP_B], False)
+    finish(0, [18 + DEP_A], False)
 
     for slot in pending:
         for c in copies(pending[slot]):
             c.wait_send()
     p_steps[8]()
     b_steps[8]()
-    pltpu.make_async_copy(uout, upd_hbm, out_sem.at[0]).wait()
-    pltpu.make_async_copy(fb, new_hbm, out_sem.at[1]).wait()
 
 
 def small_buffers(length):
@@ -617,15 +634,16 @@
 
 def on_device(layer_input, up_cotangent, attn_values, resid_cotangent, feedback, start_seed):
     hbm = pl.BlockSpec(memory_space=pl.ANY)
+    vmem = pl.BlockSpec(memory_space=pltpu.VMEM)
     dma = pltpu.SemaphoreType.DMA
     new_feedback, update = pl.pallas_call(
         kernel,
         out_shape=(
-            jax.ShapeDtypeStruct((ROWS, W), F32),
-            jax.ShapeDtypeStruct((W // REP, D), BF16),
+            pltpu.VMEM((ROWS, W), F32),
+            pltpu.VMEM((W // REP, D), BF16),
         ),
         in_specs=[hbm] * 5 + [pl.BlockSpec(memory_space=pltpu.SMEM)],
-        out_specs=(hbm, hbm),
+        out_specs=(vmem, vmem),
         scratch_shapes=[
             pltpu.VMEM((SIDE, TOK, SIDE * ROWS), BF16),
             pltpu.VMEM((SIDE, TOK, SIDE * ROWS), BF16),
@@ -636,24 +654,21 @@
             pltpu.VMEM((W, ROWS), F32),
             pltpu.VMEM((14, HALF + 16, ROWS), jnp.int16),
             pltpu.VMEM((30, HALF + 16, ROWS), jnp.int16),
-            pltpu.VMEM((ROWS, W), F32),
             pltpu.VMEM((96, W), BF16),
             *small_buffers(D),
             *small_buffers(BLEN),
             pltpu.VMEM((W, 256), BF16),
-            pltpu.VMEM((W // REP, D), BF16),
             dma((GROUP,)),
             dma((GROUP,)),
             dma((3,)),
             dma,
-            dma((2,)),
             dma((30, 2)),
             dma((30, 2)),
             dma((14,)),
             dma((14,)),
         ],
         compiler_params=pltpu.CompilerParams(
-            collective_id=0, has_side_effects=True, vmem_limit_bytes=64 * 1024 * 1024 - 256 * 1024
+            collective_id=0, has_side_effects=True, vmem_limit_bytes=58 * 1024 * 1024
         ),
         cost_estimate=pl.CostEstimate(flops=2 * TOK * D * W, bytes_accessed=21_000_000, transcendentals=0),
     )(layer_input, up_cotangent, attn_values, resid_cotangent, feedback[0], start_seed)

time: 124 us -> 118 us (0.952)
  Pallas kernels: 118 us -> 113 us
  local copies, waits for them, and re-layouts: 4.88 us -> 2.81 us
    pallas_call x1, Pallas kernels: 118 us -> 113 us  [on_device(): pl.pallas_call(kernel, out_shape=(pltpu.VMEM((ROWS, W), F32), pltpu.VMEM(...]
    unnamed x4 -> x2, local copies, waits for them, and re-layouts: 4.88 us -> 2.81 us
where the time goes in v4:
time: 118 us; the launch traced here: 117 us
  Pallas kernels  113 us (96%)
  local copies, waits for them, and re-layouts  2.81 us (2%)
  between operations  1.29 us (1%)
    pallas_call x1, Pallas kernels, on_device(): pl.pallas_call(kernel, out_shape=(pltpu.VMEM((ROWS, W), F32), pltpu.VMEM(...  113 us
    unnamed x2, local copies, waits for them, and re-layouts  2.81 us

profile of v4, /device:TPU:0, one launch (start us, length us, event | category | flops | bytes accessed | tf_op | source)
XLA Modules:
  0.0 117.2 jit_solution(2157466774311916570)
XLA Ops:
  1.3 113.1 %shard_map.77 = (f32[256,2304]{1,0:T(8,128)S(1)}, bf16[288,4096]{1,0:T(8,128)(2,1)S(1)}) custom-call(bf16[768,4096]{1,0:T(8,128)(2,1)} %x_hbm.1, bf16[768,1792]{1,0:T(8,128)(2,1)} %u_hbm.1, bf16[768,512]{1,0:T(8,128)(2,1)} %a_hbm.1, bf16[768,4096]{1,0:T(8,128)(2,1)} %g_hbm.1, f32[256,2304]{1,0:T(8,128)} %bitcast.5, s32[1]{0:T(128)S(6)} %copy.12.seed_ref), custom_call_target="tpu_custom_call" | custom-call | flops 14495514624 | bytes 21000000 | tf_op jit(solution)/shard_map/pallas_call | solution.py:639
  114.4 1.4 %copy.10 = bf16[4096,288]{0,1:T(8,128)(2,1)} copy(bf16[4096,288]{0,1:T(8,128)(2,1)S(1)} %bitcast.4) | data formatting | bytes 4718592
  115.8 1.4 %copy.11 = f32[1,256,2304]{2,1,0:T(8,128)} copy(f32[1,256,2304]{2,1,0:T(8,128)S(1)} %bitcast.3) | data formatting | bytes 4718592

commit v5 on v4

--- a/solution.py
+++ b/solution.py
@@ -552,18 +552,18 @@
     pure_b(0)
     pure_a(0)
     make_factors()
+    opposite_b(1)
     for k in range(SIDE):
         for j in range(SIDE):
             wait_step(k, j)
     pltpu.make_async_copy(fb_hbm, fb, load_fb).wait()
     project()
     p_steps[0]()
+    opposite_a(1)
+    dependent_a(0)
+    p_steps[1]()
+    dependent_b(0)
     own(0)
-    p_steps[1]()
-    opposite_a(1)
-    opposite_b(1)
-    dependent_a(0)
-    dependent_b(0)
     pure_b(1)
     pure_a(1)
     p_steps[2]()
@@ -607,8 +607,8 @@
     own(3)
     dependent_b(3)
     b_steps[5]()
+    dependent_a(3)
     b_steps[6]()
-    dependent_a(3)
     finish(0, [18 + PURE_A, 24 + DEP_A, 24 + PURE_A], True)
     finish(HALF, [18 + PURE_B, 24 + PURE_B, 24 + DEP_B], True)
     b_steps[7]()

time: 118 us -> 117 us (level)
  no operation moved by 1% of the time
where the time goes in v5:
time: 117 us
  Pallas kernels  113 us (97%)
  local copies, waits for them, and re-layouts  2.81 us (2%)
  between operations  1.29 us (1%)
    pallas_call x1, Pallas kernels, on_device(): pl.pallas_call(kernel, out_shape=(pltpu.VMEM((ROWS, W), F32), pltpu.VMEM(...  113 us
    unnamed x2, local copies, waits for them, and re-layouts  2.81 us

profile of v5, /device:TPU:0, one launch (start us, length us, event | category | flops | bytes accessed | tf_op | source)
XLA Modules:
  0.0 117.2 jit_solution(8706690988159881269)
XLA Ops:
  1.3 113.1 %shard_map.77 = (f32[256,2304]{1,0:T(8,128)S(1)}, bf16[288,4096]{1,0:T(8,128)(2,1)S(1)}) custom-call(bf16[768,4096]{1,0:T(8,128)(2,1)} %x_hbm.1, bf16[768,1792]{1,0:T(8,128)(2,1)} %u_hbm.1, bf16[768,512]{1,0:T(8,128)(2,1)} %a_hbm.1, bf16[768,4096]{1,0:T(8,128)(2,1)} %g_hbm.1, f32[256,2304]{1,0:T(8,128)} %bitcast.5, s32[1]{0:T(128)S(6)} %copy.12.seed_ref), custom_call_target="tpu_custom_call" | custom-call | flops 14495514624 | bytes 21000000 | tf_op jit(solution)/shard_map/pallas_call | solution.py:639
  114.4 1.4 %copy.10 = bf16[4096,288]{0,1:T(8,128)(2,1)} copy(bf16[4096,288]{0,1:T(8,128)(2,1)S(1)} %bitcast.4) | data formatting | bytes 4718592
  115.8 1.4 %copy.11 = f32[1,256,2304]{2,1,0:T(8,128)} copy(f32[1,256,2304]{2,1,0:T(8,128)S(1)} %bitcast.3) | data formatting | bytes 4718592

commit v6 on v5

--- a/solution.py
+++ b/solution.py
@@ -538,6 +538,7 @@
 
     load_step(0, 1)
     load_step(0, 2)
+    make_factors()
     load_a.wait()
     transpose_u(0, (384, 384, 384))
     load_b.start()
@@ -551,7 +552,6 @@
     opposite_b(0)
     pure_b(0)
     pure_a(0)
-    make_factors()
     opposite_b(1)
     for k in range(SIDE):
         for j in range(SIDE):

time: 117 us -> 117 us (level)
  no operation moved by 1% of the time
where the time goes in v6:
time: 117 us
  Pallas kernels  113 us (97%)
  local copies, waits for them, and re-layouts  2.81 us (2%)
  between operations  1.29 us (1%)
    pallas_call x1, Pallas kernels, on_device(): pl.pallas_call(kernel, out_shape=(pltpu.VMEM((ROWS, W), F32), pltpu.VMEM(...  113 us
    unnamed x2, local copies, waits for them, and re-layouts  2.81 us

profile of v6, /device:TPU:0, one launch (start us, length us, event | category | flops | bytes accessed | tf_op | source)
XLA Modules:
  0.0 117.2 jit_solution(8341609681956329138)
XLA Ops:
  1.3 113.1 %shard_map.77 = (f32[256,2304]{1,0:T(8,128)S(1)}, bf16[288,4096]{1,0:T(8,128)(2,1)S(1)}) custom-call(bf16[768,4096]{1,0:T(8,128)(2,1)} %x_hbm.1, bf16[768,1792]{1,0:T(8,128)(2,1)} %u_hbm.1, bf16[768,512]{1,0:T(8,128)(2,1)} %a_hbm.1, bf16[768,4096]{1,0:T(8,128)(2,1)} %g_hbm.1, f32[256,2304]{1,0:T(8,128)} %bitcast.5, s32[1]{0:T(128)S(6)} %copy.12.seed_ref), custom_call_target="tpu_custom_call" | custom-call | flops 14495514624 | bytes 21000000 | tf_op jit(solution)/shard_map/pallas_call | solution.py:639
  114.4 1.4 %copy.10 = bf16[4096,288]{0,1:T(8,128)(2,1)} copy(bf16[4096,288]{0,1:T(8,128)(2,1)S(1)} %bitcast.4) | data formatting | bytes 4718592
  115.8 1.4 %copy.11 = f32[1,256,2304]{2,1,0:T(8,128)} copy(f32[1,256,2304]{2,1,0:T(8,128)S(1)} %bitcast.3) | data formatting | bytes 4718592
